TPU v7x, 512 devices: a whole 4x8x8 slice. The times are simulated.
512 devices in a mesh: inp: 64 (over x, y, core), tm: 8 (over z).
Axes of the slice: x: 4, y: 8, z: 8, core: 2. Of those that a mesh axis runs over, the one named last changes fastest.
Arguments:
- volts: bfloat16 [512, 524288], P('inp', 'tm'), may hold values from -6 to 6
Outputs:
- visibilities: float32 [2, 512, 512, 512], P(None, ('inp', 'tm'))
All inputs are finite; a program needn't handle non-finite values.
Results may differ from a plain program's by a relative error of at most 0.0047.
Values may be sent and summed in bfloat16 or wider, within the bound.
No kernel may reach another device: no remote copies, remote signals or barrier semaphores. Data moves between devices by JAX's collectives and lax.ppermute only.
A program may use at most 64 MiB of HBM per device.

v0:
```python
import math

import jax
import jax.numpy as jnp
from jax import lax
from jax.sharding import PartitionSpec as P

FFT = 1024
TAPS = 4
CHAN = 512


def shifted_2(array, axis, by):
    size = lax.axis_size(axis)
    pairs = [(i, i + by) for i in range(size) if 0 <= i + by < size]
    return lax.ppermute(array, axis, pairs)


def filter_taps():
    position = jnp.arange(TAPS * FFT, dtype=jnp.float32)
    shifted = (position + 0.5) / FFT - TAPS / 2
    sinc_part = jnp.sin(jnp.pi * shifted) / (jnp.pi * shifted)
    window = 0.54 - 0.46 * jnp.cos(2.0 * jnp.pi * (position + 0.5) / (TAPS * FFT))
    return (sinc_part * window).reshape(TAPS, FFT)


def twiddle_table(channel_order):
    samples = jnp.arange(FFT, dtype=jnp.int32)
    phase = samples[:, None] * channel_order[None, :] % FFT
    angle = phase.astype(jnp.float32) * (2.0 * math.pi / FFT)
    scale = 1.0 / math.sqrt(FFT)
    return jnp.stack([jnp.cos(angle) * scale, -jnp.sin(angle) * scale], axis=1).astype(jnp.bfloat16)


def polyphase(extended, coeff):
    spectra_count = extended.shape[1] - (TAPS - 1)
    total = coeff[0][None, None, :] * extended[:, 0:spectra_count, :].astype(jnp.float32)
    for step in range(1, TAPS):
        total = total + coeff[step][None, None, :] * extended[
            :, step : step + spectra_count, :
        ].astype(jnp.float32)
    return total.astype(jnp.bfloat16)


def cross_block(left_part, right_part, time_total):
    gram = jnp.einsum("qkat,pkbt->qpkab", left_part, right_part, preferred_element_type=jnp.float32)
    real_part = (gram[0, 0] + gram[1, 1]) / time_total
    imag_part = (gram[1, 0] - gram[0, 1]) / time_total
    return (real_part, imag_part)


def on_device(volts):
    inp_local = volts.shape[0]
    spectra_count = volts.shape[1] // FFT
    blocks = volts.reshape(inp_local, spectra_count, FFT)
    earlier = shifted_2(blocks[:, spectra_count - (TAPS - 1) :, :], "tm", 1)
    extended = jnp.concatenate([earlier, blocks], axis=1)
    filtered = polyphase(extended, filter_taps())
    natural_order = jnp.arange(CHAN, dtype=jnp.int32)
    table = twiddle_table(natural_order)
    spectra = jnp.einsum(
        "isn,nqc->qcis", filtered, table, preferred_element_type=jnp.float32
    ).astype(jnp.bfloat16)
    turned = lax.all_to_all(
        lax.all_to_all(spectra, "inp", split_axis=1, concat_axis=2, tiled=True),
        "tm",
        split_axis=1,
        concat_axis=3,
        tiled=True,
    )
    time_total = turned.shape[3]
    real_part, imag_part = cross_block(turned, turned, time_total)
    return jnp.stack([real_part, imag_part])


def solution(mesh):
    placed = (P("inp", "tm"),)
    return jax.shard_map(
        on_device,
        mesh=mesh,
        in_specs=placed,
        out_specs=P(None, ("inp", "tm"), None, None),
        check_vma=False,
    )
```

profile of v0, /device:TPU:1, one launch (start us, length us, event | category | flops | bytes accessed | tf_op | source)
XLA Modules:
  0.0 109.6 jit_solution(3202722655845068946)
XLA Ops:
  0.0 1.8 %copy.20 = bf16[8,64,1024]{2,1,0:T(8,128)(2,1)S(1)} copy(bf16[8,64,1024]{2,0,1:T(8,128)(2,1)} %bitcast.58) | data formatting | bytes 2097152 | tf_op jit(solution)/shard_map/reshape | solution.py:55
  1.9 4.8 %collective-permute-start = (bf16[8,3,1024]{2,1,0:T(4,128)(2,1)S(1)}, bf16[8,3,1024]{2,1,0:T(4,128)(2,1)S(1)}, u32[]{:S(2)}, u32[]{:S(2)}) collective-permute-start(bf16[8,3,1024]{2,1,0:T(4,128)(2,1)S(1)} %slice.53), channel_id=1, source_target_pairs={{0,1},{1,2},{2,3},{3,4},{4,5},{5,6},{6,7},{8,9},{9,10},{10,11},{11... | collective-permute-start | bytes 147464 | tf_op jit(solution)/shard_map/ppermute | solution.py:16
  6.7 0.1 fusion.21
  6.8 8.6 %multiply_convert_fusion = (bf16[1024,1,512]{2,0,1:T(8,128)(2,1)S(1)}, bf16[1024,1,512]{2,0,1:T(8,128)(2,1)S(1)}) fusion(), kind=kLoop, calls=%fused_computation.14 | loop fusion | flops 9961472 | bytes 2097152 | tf_op jit(solution)/shard_map/convert.1
  15.5 0.0 collective-permute-done
  15.5 1.6 %fusion.9 = bf16[2,512,8,64]{1,3,2,0:T(8,128)(2,1)S(1)} fusion(bf16[1024,1,512]{2,0,1:T(8,128)(2,1)S(1)} %get-tuple-element.9, bf16[1024,1,512]{2,0,1:T(8,128)(2,1)S(1)} %get-tuple-element.10, bf16[8,64,1024]{2,1,0:T(8,128)(2,1)S(1)} %copy.20, bf16[8,3,1024]{2,1,0:T(4,128)(2,1)S(1)} %collective-permute-done, f32[1024]{0:T(1024)S(1)} %get-tuple-element.6, ...), kind=kOutput, calls=%fused_computation.21 | convolution fusion | flops 1089470464 | bytes 4259840 | tf_op jit(solution)/shard_map/isn,nqc->qcis/dot_general | solution.py:61
  17.0 2.0 %copy.23 = bf16[2,512,8,64]{3,2,0,1:T(8,128)(2,1)S(1)} copy(bf16[2,512,8,64]{1,3,2,0:T(8,128)(2,1)S(1)} %fusion.9) | data formatting | bytes 2097152 | tf_op jit(solution)/shard_map/convert_element_type | solution.py:63
  19.1 1.5 %reshape.164 = bf16[64,2,4096]{2,1,0:T(2,128)(2,1)S(1)} reshape(bf16[512,2,8,64]{3,2,1,0:T(8,128)(2,1)S(1)} %bitcast.55) | data formatting | bytes 2097152
  20.6 39.5 %all_to_all.33 = bf16[64,2,4096]{2,1,0:T(2,128)(2,1)} all-to-all(bf16[64,2,4096]{2,1,0:T(2,128)(2,1)S(1)} %reshape.164), channel_id=1, replica_groups=mesh['inp'=64,'tm'=8] {'inp'}, dimensions={0} | all-to-all | bytes 2097152 | tf_op jit(solution)/shard_map/all_to_all | solution.py:65
  60.1 3.8 %reshape.165 = bf16[512,2,8,64]{3,2,1,0:T(8,128)(2,1)S(1)} reshape(bf16[64,2,4096]{2,1,0:T(2,128)(2,1)} %all_to_all.33) | data formatting | bytes 2097152
  63.9 1.9 %copy.45 = bf16[2,8,64,8,64]{4,3,2,1,0:T(8,128)(2,1)} copy(bf16[2,8,64,8,64]{4,3,0,1,2:T(8,128)(2,1)S(1)} %bitcast.56) | data formatting | bytes 2097152 | tf_op jit(solution)/shard_map/all_to_all | solution.py:65
  65.8 1.9 %copy.26 = bf16[2,8,512,64]{2,3,0,1:T(8,128)(2,1)S(1)} copy(bf16[2,8,512,64]{3,2,1,0:T(8,128)(2,1)} %bitcast.57) | data formatting | bytes 2097152 | tf_op jit(solution)/shard_map/all_to_all | solution.py:65
  67.7 38.2 %all_to_all.34 = bf16[2,8,512,64]{2,3,0,1:T(8,128)(2,1)S(1)} all-to-all(bf16[2,8,512,64]{2,3,0,1:T(8,128)(2,1)S(1)} %copy.26), channel_id=1, replica_groups=mesh['inp'=64,'tm'=8] {'tm'}, dimensions={1} | all-to-all | bytes 2097152 | tf_op jit(solution)/shard_map/all_to_all | solution.py:64
  105.8 1.3 %convolution_bitcast_fusion = f32[2,2,1,512,512]{3,4,0,1,2:T(8,128)S(1)} fusion(bf16[2,8,512,64]{2,3,0,1:T(8,128)(2,1)S(1)} %all_to_all.34), kind=kOutput, calls=%fused_computation.3 | convolution fusion | flops 1073741824 | bytes 5242880 | tf_op jit(solution)/shard_map/qkat,pkbt->qpkab/dot_general | solution.py:46
  107.1 0.2 fusion.13
  107.3 0.2 fusion.16
  107.6 0.2 pad_maximum_fusion
  107.8 1.8 %copy.31 = f32[2,1,512,512]{3,2,1,0:T(8,128)} copy(f32[2,1,512,512]{2,3,1,0:T(8,128)S(1)} %pad_maximum_fusion) | data formatting | bytes 4194304 | tf_op jit(solution)/shard_map/stack | solution.py:73
  (2 shorter events, 0.0 us)
Async XLA Ops:
  1.9 13.6 %collective-permute-start = (bf16[8,3,1024]{2,1,0:T(4,128)(2,1)S(1)}, bf16[8,3,1024]{2,1,0:T(4,128)(2,1)S(1)}, u32[]{:S(2)}, u32[]{:S(2)}) collective-permute-start(bf16[8,3,1024]{2,1,0:T(4,128)(2,1)S(1)} %slice.53), channel_id=1, source_target_pairs={{0,1},{1,2},{2,3},{3,4},{4,5},{5,6},{6,7},{8,9},{9,10},{10,11},{11... | collective-permute-start | bytes 147464 | tf_op jit(solution)/shard_map/ppermute | solution.py:16
where the time goes:
time: 110 us
  blocking collectives  77.7 us (71%)
  local copies, waits for them, and re-layouts  14.7 us (13%)
  other arithmetic  9.37 us (9%)
  starting transfers between devices  4.83 us (4%)
  matrix products  2.84 us (3%)
    all_to_all x1, blocking collectives, on_device(): lax.all_to_all(spectra, 'inp', split_axis=1, concat_axis=2, tiled=True)  39.5 us
    all_to_all x1, blocking collectives, on_device(): lax.all_to_all(lax.all_to_all(spectra, 'inp', split_axis=1, concat_axis=2...  38.2 us
    another operation x1, other arithmetic  8.61 us
    unnamed x2, local copies, waits for them, and re-layouts  5.28 us
    ppermute x1, starting transfers between devices, shifted_2(): return lax.ppermute(array, axis, pairs)  4.83 us
    all_to_all x2, local copies, waits for them, and re-layouts, on_device(): lax.all_to_all(spectra, 'inp', split_axis=1, concat_axis=2, tiled=True)  3.77 us
  transfers between devices with their start and end apart: 1, of which 0 were waited for; matrix products, arithmetic and copies ran while one was open for 8% of the time, Pallas kernels for 0%

commit v1 on v0

v1 whole, which is shorter than its diff:
```python
import functools
import math

import jax
import jax.numpy as jnp
from jax import lax
from jax.experimental import pallas as pl
from jax.experimental.pallas import tpu as pltpu
from jax.sharding import PartitionSpec as P

FFT = 1024
TAPS = 4
CHAN = 512
LANES = 128
ROWS = 8
VMEM_LIMIT = 40 * 1024 * 1024
NT = (((1,), (1,)), ((), ()))


def table_kernel(tab_ref, coef_ref, ecos_ref, esin_ref):
    position = (
        lax.broadcasted_iota(jnp.int32, (TAPS, FFT), 0) * FFT
        + lax.broadcasted_iota(jnp.int32, (TAPS, FFT), 1)
    ).astype(jnp.float32)
    shifted = (position + 0.5) / FFT - TAPS / 2
    sinc_part = jnp.sin(jnp.pi * shifted) / (jnp.pi * shifted)
    window = 0.54 - 0.46 * jnp.cos(2.0 * jnp.pi * (position + 0.5) / (TAPS * FFT))
    coef_ref[...] = sinc_part * window

    step = 2.0 * math.pi / FFT
    scale = 1.0 / math.sqrt(FFT)
    groups = CHAN // ROWS
    phase = (
        lax.broadcasted_iota(jnp.int32, (groups, LANES), 0)
        * lax.broadcasted_iota(jnp.int32, (groups, LANES), 1)
        * ROWS
    ) % FFT
    angle = phase.astype(jnp.float32) * step
    ecos_ref[...] = jnp.cos(angle)
    esin_ref[...] = jnp.sin(angle)
    sub = lax.broadcasted_iota(jnp.int32, (ROWS, LANES), 0)
    lane = lax.broadcasted_iota(jnp.int32, (ROWS, LANES), 1)
    angle = (sub * lane).astype(jnp.float32) * step
    gcos = jnp.cos(angle) * scale
    gsin = jnp.sin(angle) * scale
    turns = []
    for j in range(FFT // LANES):
        angle = ((sub * (j * LANES)) % FFT).astype(jnp.float32) * step
        turns.append((jnp.cos(angle), jnp.sin(angle)))

    def pair(p, carry):
        bases = []
        for half in range(2):
            ec = ecos_ref[pl.ds(2 * p + half, 1), :]
            es = esin_ref[pl.ds(2 * p + half, 1), :]
            bases.append((ec * gcos - es * gsin, es * gcos + ec * gsin))
        row = pl.multiple_of(p * 2 * ROWS, 2 * ROWS)
        for j, (tc, ts) in enumerate(turns):
            cols = slice(j * LANES, (j + 1) * LANES)
            real = [bc * tc - bs * ts for bc, bs in bases]
            imag = [-(bs * tc + bc * ts) for bc, bs in bases]
            tab_ref[pl.ds(row, 2 * ROWS), cols] = jnp.concatenate(real, 0).astype(jnp.bfloat16)
            tab_ref[pl.ds(CHAN + row, 2 * ROWS), cols] = jnp.concatenate(imag, 0).astype(jnp.bfloat16)
        return carry

    lax.fori_loop(0, groups // 2, pair, 0)


def make_table():
    return pl.pallas_call(
        table_kernel,
        out_shape=(
            jax.ShapeDtypeStruct((2 * CHAN, FFT), jnp.bfloat16),
            jax.ShapeDtypeStruct((TAPS, FFT), jnp.float32),
        ),
        out_specs=(pl.BlockSpec(memory_space=pltpu.VMEM), pl.BlockSpec(memory_space=pltpu.VMEM)),
        scratch_shapes=[
            pltpu.VMEM((CHAN // ROWS, LANES), jnp.float32),
            pltpu.VMEM((CHAN // ROWS, LANES), jnp.float32),
        ],
        compiler_params=pltpu.CompilerParams(vmem_limit_bytes=VMEM_LIMIT),
        cost_estimate=pl.CostEstimate(flops=4_000_000, bytes_accessed=2_100_000, transcendentals=20_000),
        name="dft_table",
    )()


def spectra_kernel(count, volts_ref, halo_ref, coef_ref, tab_ref, out_ref, part_ref, filt_ref, tile_ref):
    def column(j, carry):
        base = pl.multiple_of(j * LANES, LANES)
        taps = [
            jnp.broadcast_to(coef_ref[pl.ds(k, 1), pl.ds(base, LANES)], (ROWS, LANES)) for k in range(TAPS)
        ]
        past = [
            halo_ref[:, pl.ds(base + k * FFT, LANES)].astype(jnp.float32) for k in range(TAPS - 1)
        ]
        for s in range(count):
            past.append(volts_ref[:, pl.ds(base + s * FFT, LANES)].astype(jnp.float32))
            total = taps[0] * past[0]
            for k in range(1, TAPS):
                total = total + taps[k] * past[k]
            past = past[1:]
            part_ref[pl.ds(s, ROWS, stride=count), :] = total
        filt_ref[:, pl.ds(base, LANES)] = part_ref[...].astype(jnp.bfloat16)
        return carry

    lax.fori_loop(0, FFT // LANES, column, 0)

    chunk = 256
    low = lax.broadcasted_iota(jnp.int32, (chunk, LANES), 1) < LANES // 2
    for h in range(CHAN // chunk):
        parts = [
            lax.dot_general(
                tab_ref[q * CHAN + h * chunk : q * CHAN + (h + 1) * chunk, :],
                filt_ref[...],
                NT,
                preferred_element_type=jnp.float32,
            )
            for q in range(2)
        ]
        for j in range(ROWS // 2):
            re = parts[0][:, j * LANES : (j + 1) * LANES]
            im = parts[1][:, j * LANES : (j + 1) * LANES]
            tile_ref[pl.ds(2 * j, chunk, stride=ROWS), :] = jnp.where(low, re, pltpu.roll(im, LANES // 2, 1))
            tile_ref[pl.ds(2 * j + 1, chunk, stride=ROWS), :] = jnp.where(
                low, pltpu.roll(re, LANES // 2, 1), im
            )
        out_ref[h * chunk * ROWS : (h + 1) * chunk * ROWS, :] = tile_ref[...].astype(jnp.bfloat16)


def make_spectra(volts, halo, coef, table):
    count = volts.shape[1] // FFT
    vmem = pl.BlockSpec(memory_space=pltpu.VMEM)
    return pl.pallas_call(
        functools.partial(spectra_kernel, count),
        out_shape=jax.ShapeDtypeStruct((CHAN * ROWS, LANES), jnp.bfloat16),
        in_specs=[vmem] * 4,
        out_specs=vmem,
        scratch_shapes=[
            pltpu.VMEM((ROWS * count, LANES), jnp.float32),
            pltpu.VMEM((ROWS * count, FFT), jnp.bfloat16),
            pltpu.VMEM((256 * ROWS, LANES), jnp.float32),
        ],
        compiler_params=pltpu.CompilerParams(vmem_limit_bytes=VMEM_LIMIT),
        cost_estimate=pl.CostEstimate(flops=1_100_000_000, bytes_accessed=4_000_000, transcendentals=0),
        name="spectra",
    )(volts, halo, coef, table)


def gram_kernel(scale, block, m_ref, out_ref, turned_ref):
    step = pl.program_id(0)

    @pl.when(step == 0)
    def _():
        rows = m_ref.shape[0]
        low = lax.broadcasted_iota(jnp.int32, (rows, LANES), 1) < LANES // 2
        for k in range(m_ref.shape[1] // LANES):
            cols = slice(k * LANES, (k + 1) * LANES)
            swapped = pltpu.roll(m_ref[:, cols].astype(jnp.float32), LANES // 2, 1)
            turned_ref[:, cols] = jnp.where(low, -swapped, swapped).astype(jnp.bfloat16)

    left = m_ref[pl.ds(pl.multiple_of(step * block, block), block), :]
    out_ref[0, 0] = lax.dot_general(left, m_ref[...], NT, preferred_element_type=jnp.float32) * scale
    out_ref[1, 0] = lax.dot_general(left, turned_ref[...], NT, preferred_element_type=jnp.float32) * scale


def make_gram(m, time_total):
    inputs, depth = m.shape
    block = 128
    return pl.pallas_call(
        functools.partial(gram_kernel, 1.0 / time_total, block),
        grid=(inputs // block,),
        out_shape=jax.ShapeDtypeStruct((2, 1, inputs, inputs), jnp.float32),
        in_specs=[pl.BlockSpec((inputs, depth), lambda i: (0, 0))],
        out_specs=pl.BlockSpec((2, 1, block, inputs), lambda i: (0, 0, i, 0)),
        scratch_shapes=[pltpu.VMEM((inputs, depth), jnp.bfloat16)],
        compiler_params=pltpu.CompilerParams(vmem_limit_bytes=VMEM_LIMIT),
        cost_estimate=pl.CostEstimate(flops=1_100_000_000, bytes_accessed=3_200_000, transcendentals=0),
        name="gram",
    )(m)


def on_device(volts):
    inp_local, samples = volts.shape
    count = samples // FFT
    slabs = lax.axis_size("tm")
    groups = lax.axis_size("inp")
    halo = lax.ppermute(
        volts[:, samples - (TAPS - 1) * FFT :], "tm", [(i, i + 1) for i in range(slabs - 1)]
    )
    table, coef = make_table()
    tiles = make_spectra(volts, halo, coef, table)
    tiles = tiles.reshape(CHAN, inp_local, 2 * count)
    tiles = lax.all_to_all(tiles, ("inp", "tm"), split_axis=0, concat_axis=0, tiled=True)
    m = tiles.reshape(groups, slabs, inp_local, 2 * count).transpose(0, 2, 1, 3)
    m = m.reshape(groups * inp_local, slabs * 2 * count)
    return make_gram(m, slabs * count)


def solution(mesh):
    return jax.shard_map(
        on_device,
        mesh=mesh,
        in_specs=(P("inp", "tm"),),
        out_specs=P(None, ("inp", "tm"), None, None),
        check_vma=False,
    )
```

time: 110 us -> 72.7 us (0.66)
  blocking collectives: 77.7 us -> 56.3 us
  local copies, waits for them, and re-layouts: 14.7 us -> 2.02 us
  other arithmetic: 9.37 us -> 0 us
  Pallas kernels: 0 us -> 9.27 us
  matrix products: 2.84 us -> 0 us
    all_to_all x2 -> x1, blocking collectives: 77.7 us -> 56.3 us  [on_device(): lax.all_to_all(tiles, ('inp', 'tm'), split_axis=0, concat_axis=0, tiled=T...]
    pallas_call x0 -> x3, Pallas kernels: none -> 9.27 us  [the longest x1 4.56 us: make_gram(): pl.pallas_call(functools.partial(gram_kernel, 1.0 / time_total, block), g...]
    another operation x2 -> x0, other arithmetic: 8.78 us -> none
    unnamed x2, local copies, waits for them, and re-layouts: 5.28 us -> 1.22 us
    all_to_all x2 -> x0, local copies, waits for them, and re-layouts: 3.77 us -> none  [on_device(): lax.all_to_all(spectra, 'inp', split_axis=1, concat_axis=2, tiled=True)]
    dot_general x2 -> x0, matrix products: 2.84 us -> none  [the longest x1 1.55 us: on_device(): jnp.einsum('isn,nqc->qcis', filtered, table, preferred_element_type=jnp.f...]
    convert_element_type x1 -> x0, local copies, waits for them, and re-layouts: 2.02 us -> none  [on_device(): spectra = jnp.einsum('isn,nqc->qcis', filtered, table, preferred_element_...]
    another operation x1 -> x0, local copies, waits for them, and re-layouts: 1.81 us -> none  [on_device(): return jnp.stack([real_part, imag_part])]
  transfers between devices with their start and end apart: 1 -> 1, of which waited for: 0 -> 0; matrix products, arithmetic and copies ran while one was open for 8% -> 0% of each run, Pallas kernels for 0% -> 2%
where the time goes in v1:
time: 72.7 us; the launch traced here: 72.5 us
  blocking collectives  56.3 us (77%)
  Pallas kernels  9.27 us (13%)
  starting transfers between devices  4.82 us (7%)
  local copies, waits for them, and re-layouts  2.02 us (3%)
    all_to_all x1, blocking collectives, on_device(): lax.all_to_all(tiles, ('inp', 'tm'), split_axis=0, concat_axis=0, tiled=T...  56.3 us
    ppermute x1, starting transfers between devices, on_device(): lax.ppermute(volts[:, samples - (TAPS - 1) * FFT:], 'tm', [(i, i + 1) for...  4.82 us
    pallas_call x1, Pallas kernels, make_gram(): pl.pallas_call(functools.partial(gram_kernel, 1.0 / time_total, block), g...  4.56 us
    pallas_call x1, Pallas kernels, make_spectra(): pl.pallas_call(functools.partial(spectra_kernel, count), out_shape=jax.Sh...  3.35 us
  transfers between devices with their start and end apart: 1, of which 0 were waited for; matrix products, arithmetic and copies ran while one was open for 0% of the time, Pallas kernels for 2%

profile of v1, /device:TPU:1, one launch (start us, length us, event | category | flops | bytes accessed | tf_op | source)
XLA Modules:
  0.0 72.5 jit_solution(3425482253801475168)
XLA Ops:
  0.0 0.8 %slice.3 = bf16[8,3072]{1,0:T(8,128)(2,1)S(1)} slice(bf16[8,65536]{1,0:T(8,128)(2,1)} %volts_ref.1), slice={[0:8], [62464:65536]} | slice | bytes 98304 | tf_op jit(solution)/shard_map/slice | solution.py:188
  0.8 4.8 %collective-permute-start = (bf16[8,3072]{1,0:T(8,128)(2,1)S(1)}, bf16[8,3072]{1,0:T(8,128)(2,1)S(1)}, u32[]{:S(2)}, u32[]{:S(2)}) collective-permute-start(bf16[8,3072]{1,0:T(8,128)(2,1)S(1)} %slice.3), channel_id=1, source_target_pairs={{0,1},{1,2},{2,3},{3,4},{4,5},{5,6},{6,7},{8,9},{9,10},{10,11},{11... | collective-permute-start | bytes 147464 | tf_op jit(solution)/shard_map/ppermute | solution.py:187
  5.6 1.4 %dft_table.1 = (bf16[1024,1024]{1,0:T(8,128)(2,1)S(1)}, f32[4,1024]{1,0:T(4,128)S(1)}) custom-call(), custom_call_target="tpu_custom_call" | custom-call | flops 4000000 | bytes 2100000 | tf_op jit(solution)/shard_map/dft_table/pallas_call | solution.py:70
  7.0 0.0 collective-permute-done.halo_ref
  7.0 0.0 copy-start
  7.0 1.2 %copy-done = bf16[8,65536]{1,0:T(8,128)(2,1)S(1)} copy-done((bf16[8,65536]{1,0:T(8,128)(2,1)S(1)}, bf16[8,65536]{1,0:T(8,128)(2,1)}, u32[]{:S(2)}) %copy-start) | copy-done | bytes 1048600
  8.2 3.4 %spectra.1 = bf16[4096,128]{1,0:T(8,128)(2,1)S(1)} custom-call(bf16[8,65536]{1,0:T(8,128)(2,1)S(1)} %copy-done, bf16[8,3072]{1,0:T(8,128)(2,1)S(1)} %collective-permute-done.halo_ref, f32[4,1024]{1,0:T(4,128)S(1)} %get-tuple-element.7.coef_ref, bf16[1024,1024]{1,0:T(8,128)(2,1)S(1)} %get-tuple-element.8.tab_ref), custom_call_target="tpu_custom_call" | custom-call | flops 1100000000 | bytes 4000000 | tf_op jit(solution)/shard_map/spectra/pallas_call | solution.py:133
  11.6 56.3 %all_to_all.5 = bf16[512,8,128]{2,1,0:T(8,128)(2,1)S(1)} all-to-all(bf16[512,8,128]{2,1,0:T(8,128)(2,1)S(1)} %bitcast.6), channel_id=1, replica_groups=mesh['inp'=64,'tm'=8] {'inp','tm'}, dimensions={0} | all-to-all | bytes 2097152 | tf_op jit(solution)/shard_map/all_to_all | solution.py:193
  67.9 4.6 %gram.1 = f32[2,1,512,512]{3,2,1,0:T(8,128)} custom-call(bf16[512,1024]{1,0:T(8,128)(2,1)S(1)} %bitcast.7), custom_call_target="tpu_custom_call" | custom-call | flops 1100000000 | bytes 3200000 | tf_op jit(solution)/shard_map/gram/pallas_call | solution.py:169
Async XLA Ops:
  0.8 6.2 %collective-permute-start = (bf16[8,3072]{1,0:T(8,128)(2,1)S(1)}, bf16[8,3072]{1,0:T(8,128)(2,1)S(1)}, u32[]{:S(2)}, u32[]{:S(2)}) collective-permute-start(bf16[8,3072]{1,0:T(8,128)(2,1)S(1)} %slice.3), channel_id=1, source_target_pairs={{0,1},{1,2},{2,3},{3,4},{4,5},{5,6},{6,7},{8,9},{9,10},{10,11},{11... | collective-permute-start | bytes 147464 | tf_op jit(solution)/shard_map/ppermute | solution.py:187
  7.0 1.2 %copy-start = (bf16[8,65536]{1,0:T(8,128)(2,1)S(1)}, bf16[8,65536]{1,0:T(8,128)(2,1)}, u32[]{:S(2)}) copy-start(bf16[8,65536]{1,0:T(8,128)(2,1)} %volts_ref.1) | copy-start | bytes 3145732

commit v2 on v1

v2 whole, which is shorter than its diff:
```python
import functools
import math

import jax
import jax.numpy as jnp
from jax import lax
from jax.experimental import pallas as pl
from jax.experimental.pallas import tpu as pltpu
from jax.sharding import PartitionSpec as P

FFT = 1024
TAPS = 4
CHAN = 512
LANES = 128
ROWS = 8
LOADS = 4
VMEM_LIMIT = 40 * 1024 * 1024
NT = (((1,), (1,)), ((), ()))


def prepare_kernel(count, volts_ref, tab_ref, coef_ref, filt_ref, head_ref, local_ref, part_ref, ecos_ref, esin_ref, sem):
    loads = []
    width = volts_ref.shape[1] // LOADS
    for i in range(LOADS):
        cols = pl.ds(i * width, width)
        loads.append(pltpu.make_async_copy(volts_ref.at[:, cols], local_ref.at[:, cols], sem.at[i]))
        loads[-1].start()

    position = (
        lax.broadcasted_iota(jnp.int32, (TAPS, FFT), 0) * FFT
        + lax.broadcasted_iota(jnp.int32, (TAPS, FFT), 1)
    ).astype(jnp.float32)
    shifted = (position + 0.5) / FFT - TAPS / 2
    sinc_part = jnp.sin(jnp.pi * shifted) / (jnp.pi * shifted)
    window = 0.54 - 0.46 * jnp.cos(2.0 * jnp.pi * (position + 0.5) / (TAPS * FFT))
    coef_ref[...] = sinc_part * window

    step = 2.0 * math.pi / FFT
    scale = 1.0 / math.sqrt(FFT)
    groups = CHAN // ROWS
    phase = (
        lax.broadcasted_iota(jnp.int32, (groups, LANES), 0)
        * lax.broadcasted_iota(jnp.int32, (groups, LANES), 1)
        * ROWS
    ) % FFT
    angle = phase.astype(jnp.float32) * step
    ecos_ref[...] = jnp.cos(angle)
    esin_ref[...] = jnp.sin(angle)
    sub = lax.broadcasted_iota(jnp.int32, (ROWS, LANES), 0)
    lane = lax.broadcasted_iota(jnp.int32, (ROWS, LANES), 1)
    angle = (sub * lane).astype(jnp.float32) * step
    gcos = jnp.cos(angle) * scale
    gsin = jnp.sin(angle) * scale
    half_turns = FFT // LANES // 2
    turns = []
    for j in range(half_turns):
        angle = ((sub * (j * LANES)) % FFT).astype(jnp.float32) * step
        turns.append((jnp.cos(angle), jnp.sin(angle)))
    odd = lax.broadcasted_iota(jnp.int32, (2 * ROWS, LANES), 0) % 2 == 1
    sign = jnp.where(odd, -1.0, 1.0).astype(jnp.bfloat16)

    def pair(p, carry):
        bases = []
        for half in range(2):
            ec = ecos_ref[pl.ds(2 * p + half, 1), :]
            es = esin_ref[pl.ds(2 * p + half, 1), :]
            bases.append((ec * gcos - es * gsin, es * gcos + ec * gsin))
        row = pl.multiple_of(p * 2 * ROWS, 2 * ROWS)
        for j, (tc, ts) in enumerate(turns):
            real = [bc * tc - bs * ts for bc, bs in bases] if j else [bc for bc, bs in bases]
            imag = [-(bs * tc + bc * ts) for bc, bs in bases] if j else [-bs for bc, bs in bases]
            for q, value in enumerate((real, imag)):
                value = jnp.concatenate(value, 0).astype(jnp.bfloat16)
                rows = pl.ds(q * CHAN + row, 2 * ROWS)
                tab_ref[rows, j * LANES : (j + 1) * LANES] = value
                tab_ref[rows, (j + half_turns) * LANES : (j + half_turns + 1) * LANES] = value * sign
        return carry

    lax.fori_loop(0, groups // 2, pair, 0)

    for load in loads:
        load.wait()

    pitch = count + ROWS

    def column(j, carry):
        base = pl.multiple_of(j * LANES, LANES)
        cols = pl.ds(base, LANES)
        taps = [jnp.broadcast_to(coef_ref[pl.ds(k, 1), cols], (ROWS, LANES)) for k in range(TAPS)]
        past = []
        for s in range(count):
            past.append(local_ref[:, pl.ds(base + s * FFT, LANES)].astype(jnp.float32))
            total = taps[TAPS - len(past)] * past[0]
            for k in range(1, len(past)):
                total = total + taps[TAPS - len(past) + k] * past[k]
            if s < TAPS - 1:
                head_ref[pl.ds(s * ROWS, ROWS), cols] = total
            else:
                past = past[1:]
            part_ref[pl.ds(s, ROWS, stride=pitch), :] = total
        for a in range(ROWS):
            filt_ref[a * count : (a + 1) * count, cols] = part_ref[a * pitch : a * pitch + count, :].astype(
                jnp.bfloat16
            )
        return carry

    lax.fori_loop(0, FFT // LANES, column, 0)


def prepare(volts):
    inp_local, samples = volts.shape
    count = samples // FFT
    vmem = pl.BlockSpec(memory_space=pltpu.VMEM)
    return pl.pallas_call(
        functools.partial(prepare_kernel, count),
        out_shape=(
            jax.ShapeDtypeStruct((2 * CHAN, FFT), jnp.bfloat16),
            jax.ShapeDtypeStruct((TAPS, FFT), jnp.float32),
            jax.ShapeDtypeStruct((ROWS * count, FFT), jnp.bfloat16),
            jax.ShapeDtypeStruct(((TAPS - 1) * ROWS, FFT), jnp.float32),
        ),
        in_specs=[pl.BlockSpec(memory_space=pltpu.HBM)],
        out_specs=(vmem,) * 4,
        scratch_shapes=[
            pltpu.VMEM((ROWS, samples), jnp.bfloat16),
            pltpu.VMEM((ROWS * (count + ROWS), LANES), jnp.float32),
            pltpu.VMEM((CHAN // ROWS, LANES), jnp.float32),
            pltpu.VMEM((CHAN // ROWS, LANES), jnp.float32),
            pltpu.SemaphoreType.DMA((LOADS,)),
        ],
        compiler_params=pltpu.CompilerParams(vmem_limit_bytes=VMEM_LIMIT),
        cost_estimate=pl.CostEstimate(flops=8_000_000, bytes_accessed=1_100_000, transcendentals=20_000),
        name="prepare",
    )(pltpu.with_memory_space_constraint(volts, pltpu.HBM))


def spectra_kernel(count, halo_ref, coef_ref, tab_ref, filt_ref, head_ref, out_ref, fixed_ref, row_ref, tile_ref):
    late = TAPS - 1
    first = lax.broadcasted_iota(jnp.int32, (ROWS, LANES), 0) < late
    for j in range(FFT // LANES):
        cols = slice(j * LANES, (j + 1) * LANES)
        before = [
            halo_ref[:, k * FFT + j * LANES : k * FFT + (j + 1) * LANES].astype(jnp.float32) for k in range(late)
        ]
        for s in range(late):
            total = head_ref[s * ROWS : (s + 1) * ROWS, cols]
            for k in range(late - s):
                total = total + coef_ref[k : k + 1, cols] * before[s + k]
            row_ref[pl.ds(s, ROWS, stride=ROWS), :] = total
        for a in range(ROWS):
            own = filt_ref[a * count : a * count + 2 * ROWS, cols].astype(jnp.float32)
            top = jnp.where(first, row_ref[a * ROWS : (a + 1) * ROWS, :], own[:ROWS])
            fixed_ref[a * count : a * count + 2 * ROWS, cols] = jnp.concatenate([top, own[ROWS:]], 0).astype(
                jnp.bfloat16
            )

    chunk = 256
    low = lax.broadcasted_iota(jnp.int32, (chunk, LANES), 1) < LANES // 2
    for h in range(CHAN // chunk):
        parts = [
            lax.dot_general(
                tab_ref[q * CHAN + h * chunk : q * CHAN + (h + 1) * chunk, :],
                fixed_ref[...],
                NT,
                preferred_element_type=jnp.float32,
            )
            for q in range(2)
        ]
        for j in range(ROWS // 2):
            re = parts[0][:, j * LANES : (j + 1) * LANES]
            im = parts[1][:, j * LANES : (j + 1) * LANES]
            tile_ref[pl.ds(2 * j, chunk, stride=ROWS), :] = jnp.where(low, re, pltpu.roll(im, LANES // 2, 1))
            tile_ref[pl.ds(2 * j + 1, chunk, stride=ROWS), :] = jnp.where(
                low, pltpu.roll(re, LANES // 2, 1), im
            )
        out_ref[h * chunk * ROWS : (h + 1) * chunk * ROWS, :] = tile_ref[...].astype(jnp.bfloat16)


def make_spectra(halo, coef, table, filtered, head):
    count = filtered.shape[0] // ROWS
    vmem = pl.BlockSpec(memory_space=pltpu.VMEM)
    return pl.pallas_call(
        functools.partial(spectra_kernel, count),
        out_shape=(
            jax.ShapeDtypeStruct((CHAN * ROWS, LANES), jnp.bfloat16),
            jax.ShapeDtypeStruct(filtered.shape, jnp.bfloat16),
        ),
        in_specs=[vmem] * 5,
        out_specs=(vmem, vmem),
        input_output_aliases={3: 1},
        scratch_shapes=[
            pltpu.VMEM((ROWS * ROWS, LANES), jnp.float32),
            pltpu.VMEM((256 * ROWS, LANES), jnp.float32),
        ],
        compiler_params=pltpu.CompilerParams(vmem_limit_bytes=VMEM_LIMIT),
        cost_estimate=pl.CostEstimate(flops=1_100_000_000, bytes_accessed=4_000_000, transcendentals=0),
        name="spectra",
    )(halo, coef, table, filtered, head)[0]


def gram_kernel(scale, m_ref, out_ref, turned_ref, block_ref, sem):
    inputs, depth = m_ref.shape
    block = inputs // 2
    low = lax.broadcasted_iota(jnp.int32, (inputs, LANES), 1) < LANES // 2
    for k in range(depth // LANES):
        cols = slice(k * LANES, (k + 1) * LANES)
        swapped = pltpu.roll(m_ref[:, cols], LANES // 2, 1)
        turned_ref[:, cols] = jnp.where(low, -swapped, swapped)
    copies = []
    for i in range(2):
        rows = pl.ds(i * block, block)
        left = m_ref[rows, :]
        for part, right_ref in enumerate((m_ref, turned_ref)):
            block_ref[part, 0, rows, :] = (
                lax.dot_general(left, right_ref[...], NT, preferred_element_type=jnp.float32) * scale
            )
            copies.append(
                pltpu.make_async_copy(
                    block_ref.at[part, 0, rows], out_ref.at[part, 0, rows], sem.at[2 * i + part]
                )
            )
            copies[-1].start()
    for copy in copies:
        copy.wait()


def make_gram(m, time_total):
    inputs, depth = m.shape
    shape = (2, 1, inputs, inputs)
    return pl.pallas_call(
        functools.partial(gram_kernel, 1.0 / time_total),
        out_shape=jax.ShapeDtypeStruct(shape, jnp.float32),
        in_specs=[pl.BlockSpec(memory_space=pltpu.VMEM)],
        out_specs=pl.BlockSpec(memory_space=pl.ANY),
        scratch_shapes=[
            pltpu.VMEM((inputs, depth), jnp.bfloat16),
            pltpu.VMEM(shape, jnp.float32),
            pltpu.SemaphoreType.DMA((4,)),
        ],
        compiler_params=pltpu.CompilerParams(vmem_limit_bytes=VMEM_LIMIT),
        cost_estimate=pl.CostEstimate(flops=1_100_000_000, bytes_accessed=3_200_000, transcendentals=0),
        name="gram",
    )(m)


def on_device(volts):
    inp_local, samples = volts.shape
    count = samples // FFT
    slabs = lax.axis_size("tm")
    groups = lax.axis_size("inp")
    halo = lax.ppermute(
        volts[:, samples - (TAPS - 1) * FFT :], "tm", [(i, i + 1) for i in range(slabs - 1)]
    )
    table, coef, filtered, head = prepare(volts)
    tiles = make_spectra(halo, coef, table, filtered, head)
    tiles = tiles.reshape(CHAN, inp_local, 2 * count)
    tiles = lax.all_to_all(tiles, ("inp", "tm"), split_axis=0, concat_axis=0, tiled=True)
    m = tiles.reshape(groups, slabs, inp_local, 2 * count).transpose(0, 2, 1, 3)
    m = m.reshape(groups * inp_local, slabs * 2 * count)
    return make_gram(m, slabs * count)


def solution(mesh):
    return jax.shard_map(
        on_device,
        mesh=mesh,
        in_specs=(P("inp", "tm"),),
        out_specs=P(None, ("inp", "tm"), None, None),
        check_vma=False,
    )
```

time: 72.7 us -> 67.4 us (0.927)
  Pallas kernels: 9.27 us -> 6.01 us
  local copies, waits for them, and re-layouts: 2.02 us -> 0.8 us
  blocking collectives: 56.3 us -> 55.5 us
    pallas_call x3, Pallas kernels: 9.27 us -> 6.01 us  [the longest x1 2.18 us: prepare(): pl.pallas_call(functools.partial(prepare_kernel, count), out_shape=(jax.S...]
    unnamed x2 -> x0, local copies, waits for them, and re-layouts: 1.22 us -> none
    all_to_all x1, blocking collectives: 56.3 us -> 55.5 us  [on_device(): lax.all_to_all(tiles, ('inp', 'tm'), split_axis=0, concat_axis=0, tiled=T...]
  transfers between devices with their start and end apart: 1 -> 1, of which waited for: 0 -> 0; matrix products, arithmetic and copies ran while one was open for 0% -> 0% of each run, Pallas kernels for 2% -> 3%
where the time goes in v2:
time: 67.4 us; the launch traced here: 67.2 us
  blocking collectives  55.5 us (82%)
  Pallas kernels  6.01 us (9%)
  starting transfers between devices  4.82 us (7%)
  local copies, waits for them, and re-layouts  0.8 us (1%)
    all_to_all x1, blocking collectives, on_device(): lax.all_to_all(tiles, ('inp', 'tm'), split_axis=0, concat_axis=0, tiled=T...  55.5 us
    ppermute x1, starting transfers between devices, on_device(): lax.ppermute(volts[:, samples - (TAPS - 1) * FFT:], 'tm', [(i, i + 1) for...  4.82 us
    pallas_call x1, Pallas kernels, prepare(): pl.pallas_call(functools.partial(prepare_kernel, count), out_shape=(jax.S...  2.18 us
    pallas_call x1, Pallas kernels, make_gram(): pl.pallas_call(functools.partial(gram_kernel, 1.0 / time_total), out_shap...  2.16 us
    pallas_call x1, Pallas kernels, make_spectra(): pl.pallas_call(functools.partial(spectra_kernel, count), out_shape=(jax.S...  1.67 us
  transfers between devices with their start and end apart: 1, of which 0 were waited for; matrix products, arithmetic and copies ran while one was open for 0% of the time, Pallas kernels for 3%

profile of v2, /device:TPU:1, one launch (start us, length us, event | category | flops | bytes accessed | tf_op | source)
XLA Modules:
  0.0 67.2 jit_solution(3295797679647344087)
XLA Ops:
  0.0 0.8 %slice.3 = bf16[8,3072]{1,0:T(8,128)(2,1)S(1)} slice(bf16[8,65536]{1,0:T(8,128)(2,1)} %volts_ref.1), slice={[0:8], [62464:65536]} | slice | bytes 98304 | tf_op jit(solution)/shard_map/slice | solution.py:252
  0.8 4.8 %collective-permute-start = (bf16[8,3072]{1,0:T(8,128)(2,1)S(1)}, bf16[8,3072]{1,0:T(8,128)(2,1)S(1)}, u32[]{:S(2)}, u32[]{:S(2)}) collective-permute-start(bf16[8,3072]{1,0:T(8,128)(2,1)S(1)} %slice.3), channel_id=1, source_target_pairs={{0,1},{1,2},{2,3},{3,4},{4,5},{5,6},{6,7},{8,9},{9,10},{10,11},{11... | collective-permute-start | bytes 147464 | tf_op jit(solution)/shard_map/ppermute | solution.py:251
  5.6 2.2 %prepare.1 = (bf16[1024,1024]{1,0:T(8,128)(2,1)S(1)}, f32[4,1024]{1,0:T(4,128)S(1)}, bf16[512,1024]{1,0:T(8,128)(2,1)S(1)}, f32[24,1024]{1,0:T(8,128)S(1)}) custom-call(bf16[8,65536]{1,0:T(8,128)(2,1)} %volts_ref.1), custom_call_target="tpu_custom_call" | custom-call | flops 8000000 | bytes 1100000 | tf_op jit(solution)/shard_map/prepare/pallas_call | solution.py:114
  7.8 0.0 collective-permute-done.halo_ref
  7.8 1.7 %spectra.1 = (bf16[4096,128]{1,0:T(8,128)(2,1)S(1)}, bf16[512,1024]{1,0:T(8,128)(2,1)S(1)}) custom-call(bf16[8,3072]{1,0:T(8,128)(2,1)S(1)} %collective-permute-done.halo_ref, f32[4,1024]{1,0:T(4,128)S(1)} %get-tuple-element.10.coef_ref, bf16[1024,1024]{1,0:T(8,128)(2,1)S(1)} %get-tuple-element.11.tab_ref, ...), custom_call_target="tpu_custom_call", output_to_operand_aliasing={{1}: (3, {})} | custom-call | flops 1100000000 | bytes 4000000 | tf_op jit(solution)/shard_map/spectra/pallas_call | solution.py:182
  9.5 55.5 %all_to_all.5 = bf16[512,8,128]{2,1,0:T(8,128)(2,1)S(1)} all-to-all(bf16[512,8,128]{2,1,0:T(8,128)(2,1)S(1)} %bitcast.6), channel_id=1, replica_groups=mesh['inp'=64,'tm'=8] {'inp','tm'}, dimensions={0} | all-to-all | bytes 2097152 | tf_op jit(solution)/shard_map/all_to_all | solution.py:257
  65.0 2.2 %gram.1 = f32[2,1,512,512]{3,2,1,0:T(8,128)} custom-call(bf16[512,1024]{1,0:T(8,128)(2,1)S(1)} %bitcast.7), custom_call_target="tpu_custom_call" | custom-call | flops 1100000000 | bytes 3200000 | tf_op jit(solution)/shard_map/gram/pallas_call | solution.py:230
Async XLA Ops:
  0.8 7.0 %collective-permute-start = (bf16[8,3072]{1,0:T(8,128)(2,1)S(1)}, bf16[8,3072]{1,0:T(8,128)(2,1)S(1)}, u32[]{:S(2)}, u32[]{:S(2)}) collective-permute-start(bf16[8,3072]{1,0:T(8,128)(2,1)S(1)} %slice.3), channel_id=1, source_target_pairs={{0,1},{1,2},{2,3},{3,4},{4,5},{5,6},{6,7},{8,9},{9,10},{10,11},{11... | collective-permute-start | bytes 147464 | tf_op jit(solution)/shard_map/ppermute | solution.py:251

commit v3 on v2

--- a/solution.py
+++ b/solution.py
@@ -14,6 +14,7 @@
 LANES = 128
 ROWS = 8
 LOADS = 4
+HALF = FFT // 2
 VMEM_LIMIT = 40 * 1024 * 1024
 NT = (((1,), (1,)), ((), ()))
 
@@ -37,43 +38,45 @@
 
     step = 2.0 * math.pi / FFT
     scale = 1.0 / math.sqrt(FFT)
-    groups = CHAN // ROWS
+    groups = CHAN // 2 // ROWS
     phase = (
         lax.broadcasted_iota(jnp.int32, (groups, LANES), 0)
         * lax.broadcasted_iota(jnp.int32, (groups, LANES), 1)
-        * ROWS
+        * (2 * ROWS)
     ) % FFT
     angle = phase.astype(jnp.float32) * step
     ecos_ref[...] = jnp.cos(angle)
     esin_ref[...] = jnp.sin(angle)
     sub = lax.broadcasted_iota(jnp.int32, (ROWS, LANES), 0)
     lane = lax.broadcasted_iota(jnp.int32, (ROWS, LANES), 1)
-    angle = (sub * lane).astype(jnp.float32) * step
-    gcos = jnp.cos(angle) * scale
-    gsin = jnp.sin(angle) * scale
-    half_turns = FFT // LANES // 2
-    turns = []
-    for j in range(half_turns):
-        angle = ((sub * (j * LANES)) % FFT).astype(jnp.float32) * step
-        turns.append((jnp.cos(angle), jnp.sin(angle)))
-    odd = lax.broadcasted_iota(jnp.int32, (2 * ROWS, LANES), 0) % 2 == 1
-    sign = jnp.where(odd, -1.0, 1.0).astype(jnp.bfloat16)
-
-    def pair(p, carry):
-        bases = []
-        for half in range(2):
-            ec = ecos_ref[pl.ds(2 * p + half, 1), :]
-            es = esin_ref[pl.ds(2 * p + half, 1), :]
-            bases.append((ec * gcos - es * gsin, es * gcos + ec * gsin))
-        row = pl.multiple_of(p * 2 * ROWS, 2 * ROWS)
-        for j, (tc, ts) in enumerate(turns):
-            real = [bc * tc - bs * ts for bc, bs in bases] if j else [bc for bc, bs in bases]
-            imag = [-(bs * tc + bc * ts) for bc, bs in bases] if j else [-bs for bc, bs in bases]
-            for q, value in enumerate((real, imag)):
-                value = jnp.concatenate(value, 0).astype(jnp.bfloat16)
-                rows = pl.ds(q * CHAN + row, 2 * ROWS)
-                tab_ref[rows, j * LANES : (j + 1) * LANES] = value
-                tab_ref[rows, (j + half_turns) * LANES : (j + half_turns + 1) * LANES] = value * sign
+    factors = []
+    for p in range(2):
+        angle = (((2 * sub + p) * lane) % FFT).astype(jnp.float32) * step
+        turns = []
+        for j in range(1, HALF // LANES):
+            turn = (((2 * sub + p) * (j * LANES)) % FFT).astype(jnp.float32) * step
+            turns.append((jnp.cos(turn), jnp.sin(turn)))
+        factors.append((jnp.cos(angle) * scale, jnp.sin(angle) * scale, turns))
+
+    def pair(r, carry):
+        starts = [
+            (ecos_ref[pl.ds(2 * r + half, 1), :], esin_ref[pl.ds(2 * r + half, 1), :]) for half in range(2)
+        ]
+        for p, (gcos, gsin, turns) in enumerate(factors):
+            bases = [(ec * gcos - es * gsin, es * gcos + ec * gsin) for ec, es in starts]
+            for j in range(HALF // LANES):
+                if j:
+                    tc, ts = turns[j - 1]
+                    real = [bc * tc - bs * ts for bc, bs in bases]
+                    imag = [-(bs * tc + bc * ts) for bc, bs in bases]
+                else:
+                    real = [bc for bc, bs in bases]
+                    imag = [-bs for bc, bs in bases]
+                for q, value in enumerate((real, imag)):
+                    row = pl.multiple_of((2 * p + q) * (CHAN // 2) + r * 2 * ROWS, 2 * ROWS)
+                    tab_ref[pl.ds(row, 2 * ROWS), j * LANES : (j + 1) * LANES] = jnp.concatenate(
+                        value, 0
+                    ).astype(jnp.bfloat16)
         return carry
 
     lax.fori_loop(0, groups // 2, pair, 0)
@@ -85,26 +88,33 @@
 
     def column(j, carry):
         base = pl.multiple_of(j * LANES, LANES)
-        cols = pl.ds(base, LANES)
-        taps = [jnp.broadcast_to(coef_ref[pl.ds(k, 1), cols], (ROWS, LANES)) for k in range(TAPS)]
-        past = []
+        cols = [pl.ds(base + h * HALF, LANES) for h in range(2)]
+        taps = [
+            [jnp.broadcast_to(coef_ref[pl.ds(k, 1), col], (ROWS, LANES)) for k in range(TAPS)] for col in cols
+        ]
+        past = [[], []]
         for s in range(count):
-            past.append(local_ref[:, pl.ds(base + s * FFT, LANES)].astype(jnp.float32))
-            total = taps[TAPS - len(past)] * past[0]
-            for k in range(1, len(past)):
-                total = total + taps[TAPS - len(past) + k] * past[k]
-            if s < TAPS - 1:
-                head_ref[pl.ds(s * ROWS, ROWS), cols] = total
-            else:
-                past = past[1:]
-            part_ref[pl.ds(s, ROWS, stride=pitch), :] = total
-        for a in range(ROWS):
-            filt_ref[a * count : (a + 1) * count, cols] = part_ref[a * pitch : a * pitch + count, :].astype(
+            total = []
+            for h in range(2):
+                past[h].append(local_ref[:, pl.ds(base + s * FFT + h * HALF, LANES)].astype(jnp.float32))
+                have = len(past[h])
+                value = taps[h][TAPS - have] * past[h][0]
+                for k in range(1, have):
+                    value = value + taps[h][TAPS - have + k] * past[h][k]
+                total.append(value)
+                if s < TAPS - 1:
+                    head_ref[pl.ds(s * ROWS, ROWS), cols[h]] = value
+                else:
+                    past[h] = past[h][1:]
+            part_ref[pl.ds(s, ROWS, stride=pitch), :] = total[0] + total[1]
+            part_ref[pl.ds(ROWS * pitch + s, ROWS, stride=pitch), :] = total[0] - total[1]
+        for a in range(2 * ROWS):
+            filt_ref[a * count : (a + 1) * count, cols[0]] = part_ref[a * pitch : a * pitch + count, :].astype(
                 jnp.bfloat16
             )
         return carry
 
-    lax.fori_loop(0, FFT // LANES, column, 0)
+    lax.fori_loop(0, HALF // LANES, column, 0)
 
 
 def prepare(volts):
@@ -114,18 +124,18 @@
     return pl.pallas_call(
         functools.partial(prepare_kernel, count),
         out_shape=(
-            jax.ShapeDtypeStruct((2 * CHAN, FFT), jnp.bfloat16),
+            jax.ShapeDtypeStruct((2 * CHAN, HALF), jnp.bfloat16),
             jax.ShapeDtypeStruct((TAPS, FFT), jnp.float32),
-            jax.ShapeDtypeStruct((ROWS * count, FFT), jnp.bfloat16),
+            jax.ShapeDtypeStruct((2 * ROWS * count, HALF), jnp.bfloat16),
             jax.ShapeDtypeStruct(((TAPS - 1) * ROWS, FFT), jnp.float32),
         ),
         in_specs=[pl.BlockSpec(memory_space=pltpu.HBM)],
         out_specs=(vmem,) * 4,
         scratch_shapes=[
             pltpu.VMEM((ROWS, samples), jnp.bfloat16),
-            pltpu.VMEM((ROWS * (count + ROWS), LANES), jnp.float32),
-            pltpu.VMEM((CHAN // ROWS, LANES), jnp.float32),
-            pltpu.VMEM((CHAN // ROWS, LANES), jnp.float32),
+            pltpu.VMEM((2 * ROWS * (count + ROWS), LANES), jnp.float32),
+            pltpu.VMEM((CHAN // 2 // ROWS, LANES), jnp.float32),
+            pltpu.VMEM((CHAN // 2 // ROWS, LANES), jnp.float32),
             pltpu.SemaphoreType.DMA((LOADS,)),
         ],
         compiler_params=pltpu.CompilerParams(vmem_limit_bytes=VMEM_LIMIT),
@@ -137,47 +147,58 @@
 def spectra_kernel(count, halo_ref, coef_ref, tab_ref, filt_ref, head_ref, out_ref, fixed_ref, row_ref, tile_ref):
     late = TAPS - 1
     first = lax.broadcasted_iota(jnp.int32, (ROWS, LANES), 0) < late
-    for j in range(FFT // LANES):
+    for j in range(HALF // LANES):
         cols = slice(j * LANES, (j + 1) * LANES)
-        before = [
-            halo_ref[:, k * FFT + j * LANES : k * FFT + (j + 1) * LANES].astype(jnp.float32) for k in range(late)
-        ]
+        totals = []
+        for h in range(2):
+            base = h * HALF + j * LANES
+            before = [
+                halo_ref[:, k * FFT + base : k * FFT + base + LANES].astype(jnp.float32) for k in range(late)
+            ]
+            for s in range(late):
+                total = head_ref[s * ROWS : (s + 1) * ROWS, base : base + LANES]
+                for k in range(late - s):
+                    total = total + coef_ref[k : k + 1, base : base + LANES] * before[s + k]
+                totals.append(total)
         for s in range(late):
-            total = head_ref[s * ROWS : (s + 1) * ROWS, cols]
-            for k in range(late - s):
-                total = total + coef_ref[k : k + 1, cols] * before[s + k]
-            row_ref[pl.ds(s, ROWS, stride=ROWS), :] = total
-        for a in range(ROWS):
+            row_ref[pl.ds(s, ROWS, stride=ROWS), :] = totals[s] + totals[late + s]
+            row_ref[pl.ds(ROWS * ROWS + s, ROWS, stride=ROWS), :] = totals[s] - totals[late + s]
+        for a in range(2 * ROWS):
             own = filt_ref[a * count : a * count + 2 * ROWS, cols].astype(jnp.float32)
             top = jnp.where(first, row_ref[a * ROWS : (a + 1) * ROWS, :], own[:ROWS])
             fixed_ref[a * count : a * count + 2 * ROWS, cols] = jnp.concatenate([top, own[ROWS:]], 0).astype(
                 jnp.bfloat16
             )
 
-    chunk = 256
+    chunk = CHAN // 2
     low = lax.broadcasted_iota(jnp.int32, (chunk, LANES), 1) < LANES // 2
-    for h in range(CHAN // chunk):
+    for p in range(2):
         parts = [
             lax.dot_general(
-                tab_ref[q * CHAN + h * chunk : q * CHAN + (h + 1) * chunk, :],
-                fixed_ref[...],
+                tab_ref[(2 * p + q) * chunk : (2 * p + q + 1) * chunk, :],
+                fixed_ref[p * ROWS * count : (p + 1) * ROWS * count, :],
                 NT,
                 preferred_element_type=jnp.float32,
             )
             for q in range(2)
         ]
+        first_row = p * chunk * ROWS
         for j in range(ROWS // 2):
             re = parts[0][:, j * LANES : (j + 1) * LANES]
             im = parts[1][:, j * LANES : (j + 1) * LANES]
-            tile_ref[pl.ds(2 * j, chunk, stride=ROWS), :] = jnp.where(low, re, pltpu.roll(im, LANES // 2, 1))
-            tile_ref[pl.ds(2 * j + 1, chunk, stride=ROWS), :] = jnp.where(
+            tile_ref[pl.ds(first_row + 2 * j, chunk, stride=ROWS), :] = jnp.where(
+                low, re, pltpu.roll(im, LANES // 2, 1)
+            )
+            tile_ref[pl.ds(first_row + 2 * j + 1, chunk, stride=ROWS), :] = jnp.where(
                 low, pltpu.roll(re, LANES // 2, 1), im
             )
-        out_ref[h * chunk * ROWS : (h + 1) * chunk * ROWS, :] = tile_ref[...].astype(jnp.bfloat16)
+    even = tile_ref[: chunk * ROWS, :].reshape(chunk, 1, ROWS, LANES)
+    odd = tile_ref[chunk * ROWS :, :].reshape(chunk, 1, ROWS, LANES)
+    out_ref[...] = jnp.concatenate([even, odd], 1).reshape(CHAN * ROWS, LANES).astype(jnp.bfloat16)
 
 
 def make_spectra(halo, coef, table, filtered, head):
-    count = filtered.shape[0] // ROWS
+    count = filtered.shape[0] // ROWS // 2
     vmem = pl.BlockSpec(memory_space=pltpu.VMEM)
     return pl.pallas_call(
         functools.partial(spectra_kernel, count),
@@ -189,11 +210,11 @@
         out_specs=(vmem, vmem),
         input_output_aliases={3: 1},
         scratch_shapes=[
-            pltpu.VMEM((ROWS * ROWS, LANES), jnp.float32),
-            pltpu.VMEM((256 * ROWS, LANES), jnp.float32),
+            pltpu.VMEM((2 * ROWS * ROWS, LANES), jnp.float32),
+            pltpu.VMEM((CHAN * ROWS, LANES), jnp.float32),
         ],
         compiler_params=pltpu.CompilerParams(vmem_limit_bytes=VMEM_LIMIT),
-        cost_estimate=pl.CostEstimate(flops=1_100_000_000, bytes_accessed=4_000_000, transcendentals=0),
+        cost_estimate=pl.CostEstimate(flops=540_000_000, bytes_accessed=3_000_000, transcendentals=0),
         name="spectra",
     )(halo, coef, table, filtered, head)[0]
 

time: 67.4 us -> 66.8 us (level)
  no operation moved by 1% of the time
where the time goes in v3:
time: 66.8 us; the launch traced here: 66.6 us
  blocking collectives  55.6 us (83%)
  Pallas kernels  5.35 us (8%)
  starting transfers between devices  4.82 us (7%)
  local copies, waits for them, and re-layouts  0.8 us (1%)
    all_to_all x1, blocking collectives, on_device(): lax.all_to_all(tiles, ('inp', 'tm'), split_axis=0, concat_axis=0, tiled=T...  55.6 us
    ppermute x1, starting transfers between devices, on_device(): lax.ppermute(volts[:, samples - (TAPS - 1) * FFT:], 'tm', [(i, i + 1) for...  4.82 us
    pallas_call x1, Pallas kernels, make_gram(): pl.pallas_call(functools.partial(gram_kernel, 1.0 / time_total), out_shap...  2.16 us
    pallas_call x1, Pallas kernels, prepare(): pl.pallas_call(functools.partial(prepare_kernel, count), out_shape=(jax.S...  2.08 us
  transfers between devices with their start and end apart: 1, of which 0 were waited for; matrix products, arithmetic and copies ran while one was open for 0% of the time, Pallas kernels for 3%

profile of v3, /device:TPU:1, one launch (start us, length us, event | category | flops | bytes accessed | tf_op | source)
XLA Modules:
  0.0 66.6 jit_solution(16916530122655166779)
XLA Ops:
  0.0 0.8 %slice.3 = bf16[8,3072]{1,0:T(8,128)(2,1)S(1)} slice(bf16[8,65536]{1,0:T(8,128)(2,1)} %volts_ref.1), slice={[0:8], [62464:65536]} | slice | bytes 98304 | tf_op jit(solution)/shard_map/slice | solution.py:273
  0.8 4.8 %collective-permute-start = (bf16[8,3072]{1,0:T(8,128)(2,1)S(1)}, bf16[8,3072]{1,0:T(8,128)(2,1)S(1)}, u32[]{:S(2)}, u32[]{:S(2)}) collective-permute-start(bf16[8,3072]{1,0:T(8,128)(2,1)S(1)} %slice.3), channel_id=1, source_target_pairs={{0,1},{1,2},{2,3},{3,4},{4,5},{5,6},{6,7},{8,9},{9,10},{10,11},{11... | collective-permute-start | bytes 147464 | tf_op jit(solution)/shard_map/ppermute | solution.py:272
  5.6 2.1 %prepare.1 = (bf16[1024,512]{1,0:T(8,128)(2,1)S(1)}, f32[4,1024]{1,0:T(4,128)S(1)}, bf16[1024,512]{1,0:T(8,128)(2,1)S(1)}, f32[24,1024]{1,0:T(8,128)S(1)}) custom-call(bf16[8,65536]{1,0:T(8,128)(2,1)} %volts_ref.1), custom_call_target="tpu_custom_call" | custom-call | flops 8000000 | bytes 1100000 | tf_op jit(solution)/shard_map/prepare/pallas_call | solution.py:124
  7.7 0.0 collective-permute-done.halo_ref
  7.7 1.1 %spectra.1 = (bf16[4096,128]{1,0:T(8,128)(2,1)S(1)}, bf16[1024,512]{1,0:T(8,128)(2,1)S(1)}) custom-call(bf16[8,3072]{1,0:T(8,128)(2,1)S(1)} %collective-permute-done.halo_ref, f32[4,1024]{1,0:T(4,128)S(1)} %get-tuple-element.10.coef_ref, bf16[1024,512]{1,0:T(8,128)(2,1)S(1)} %get-tuple-element.11.tab_ref, ...), custom_call_target="tpu_custom_call", output_to_operand_aliasing={{1}: (3, {})} | custom-call | flops 540000000 | bytes 3000000 | tf_op jit(solution)/shard_map/spectra/pallas_call | solution.py:203
  8.8 55.6 %all_to_all.5 = bf16[512,8,128]{2,1,0:T(8,128)(2,1)S(1)} all-to-all(bf16[512,8,128]{2,1,0:T(8,128)(2,1)S(1)} %bitcast.6), channel_id=1, replica_groups=mesh['inp'=64,'tm'=8] {'inp','tm'}, dimensions={0} | all-to-all | bytes 2097152 | tf_op jit(solution)/shard_map/all_to_all | solution.py:278
  64.5 2.2 %gram.1 = f32[2,1,512,512]{3,2,1,0:T(8,128)} custom-call(bf16[512,1024]{1,0:T(8,128)(2,1)S(1)} %bitcast.7), custom_call_target="tpu_custom_call" | custom-call | flops 1100000000 | bytes 3200000 | tf_op jit(solution)/shard_map/gram/pallas_call | solution.py:251
Async XLA Ops:
  0.8 6.9 %collective-permute-start = (bf16[8,3072]{1,0:T(8,128)(2,1)S(1)}, bf16[8,3072]{1,0:T(8,128)(2,1)S(1)}, u32[]{:S(2)}, u32[]{:S(2)}) collective-permute-start(bf16[8,3072]{1,0:T(8,128)(2,1)S(1)} %slice.3), channel_id=1, source_target_pairs={{0,1},{1,2},{2,3},{3,4},{4,5},{5,6},{6,7},{8,9},{9,10},{10,11},{11... | collective-permute-start | bytes 147464 | tf_op jit(solution)/shard_map/ppermute | solution.py:272

commit v4 on v3

--- a/solution.py
+++ b/solution.py
@@ -6,6 +6,7 @@
 from jax import lax
 from jax.experimental import pallas as pl
 from jax.experimental.pallas import tpu as pltpu
+from jax.sharding import Mesh
 from jax.sharding import PartitionSpec as P
 
 FFT = 1024
@@ -14,6 +15,7 @@
 LANES = 128
 ROWS = 8
 LOADS = 4
+CORES = 2
 HALF = FFT // 2
 VMEM_LIMIT = 40 * 1024 * 1024
 NT = (((1,), (1,)), ((), ()))
@@ -49,12 +51,13 @@
     esin_ref[...] = jnp.sin(angle)
     sub = lax.broadcasted_iota(jnp.int32, (ROWS, LANES), 0)
     lane = lax.broadcasted_iota(jnp.int32, (ROWS, LANES), 1)
+    near = CORES * ROWS // 2 * (sub % CORES) + 2 * (sub // CORES)
     factors = []
     for p in range(2):
-        angle = (((2 * sub + p) * lane) % FFT).astype(jnp.float32) * step
+        angle = (((near + p) * lane) % FFT).astype(jnp.float32) * step
         turns = []
         for j in range(1, HALF // LANES):
-            turn = (((2 * sub + p) * (j * LANES)) % FFT).astype(jnp.float32) * step
+            turn = (((near + p) * (j * LANES)) % FFT).astype(jnp.float32) * step
             turns.append((jnp.cos(turn), jnp.sin(turn)))
         factors.append((jnp.cos(angle) * scale, jnp.sin(angle) * scale, turns))
 
@@ -192,8 +195,9 @@
             tile_ref[pl.ds(first_row + 2 * j + 1, chunk, stride=ROWS), :] = jnp.where(
                 low, pltpu.roll(re, LANES // 2, 1), im
             )
-    even = tile_ref[: chunk * ROWS, :].reshape(chunk, 1, ROWS, LANES)
-    odd = tile_ref[chunk * ROWS :, :].reshape(chunk, 1, ROWS, LANES)
+    pairs = (chunk // CORES, 1, CORES * ROWS, LANES)
+    even = tile_ref[: chunk * ROWS, :].reshape(pairs)
+    odd = tile_ref[chunk * ROWS :, :].reshape(pairs)
     out_ref[...] = jnp.concatenate([even, odd], 1).reshape(CHAN * ROWS, LANES).astype(jnp.bfloat16)
 
 
@@ -219,13 +223,15 @@
     )(halo, coef, table, filtered, head)[0]
 
 
-def gram_kernel(scale, m_ref, out_ref, turned_ref, block_ref, sem):
+def gram_kernel(scale, tiles_ref, out_ref, m_ref, turned_ref, block_ref, sem):
     inputs, depth = m_ref.shape
     block = inputs // 2
     low = lax.broadcasted_iota(jnp.int32, (inputs, LANES), 1) < LANES // 2
     for k in range(depth // LANES):
         cols = slice(k * LANES, (k + 1) * LANES)
-        swapped = pltpu.roll(m_ref[:, cols], LANES // 2, 1)
+        tile = tiles_ref[:, k].reshape(inputs, LANES)
+        m_ref[:, cols] = tile
+        swapped = pltpu.roll(tile, LANES // 2, 1)
         turned_ref[:, cols] = jnp.where(low, -swapped, swapped)
     copies = []
     for i in range(2):
@@ -245,8 +251,9 @@
         copy.wait()
 
 
-def make_gram(m, time_total):
-    inputs, depth = m.shape
+def make_gram(tiles, time_total):
+    chips, slabs, rows, lanes = tiles.shape
+    inputs, depth = chips * rows, slabs * lanes
     shape = (2, 1, inputs, inputs)
     return pl.pallas_call(
         functools.partial(gram_kernel, 1.0 / time_total),
@@ -255,37 +262,38 @@
         out_specs=pl.BlockSpec(memory_space=pl.ANY),
         scratch_shapes=[
             pltpu.VMEM((inputs, depth), jnp.bfloat16),
+            pltpu.VMEM((inputs, depth), jnp.bfloat16),
             pltpu.VMEM(shape, jnp.float32),
             pltpu.SemaphoreType.DMA((4,)),
         ],
         compiler_params=pltpu.CompilerParams(vmem_limit_bytes=VMEM_LIMIT),
         cost_estimate=pl.CostEstimate(flops=1_100_000_000, bytes_accessed=3_200_000, transcendentals=0),
         name="gram",
-    )(m)
+    )(tiles)
 
 
 def on_device(volts):
     inp_local, samples = volts.shape
     count = samples // FFT
     slabs = lax.axis_size("tm")
-    groups = lax.axis_size("inp")
+    chips = lax.axis_size("chip")
     halo = lax.ppermute(
         volts[:, samples - (TAPS - 1) * FFT :], "tm", [(i, i + 1) for i in range(slabs - 1)]
     )
     table, coef, filtered, head = prepare(volts)
     tiles = make_spectra(halo, coef, table, filtered, head)
     tiles = tiles.reshape(CHAN, inp_local, 2 * count)
-    tiles = lax.all_to_all(tiles, ("inp", "tm"), split_axis=0, concat_axis=0, tiled=True)
-    m = tiles.reshape(groups, slabs, inp_local, 2 * count).transpose(0, 2, 1, 3)
-    m = m.reshape(groups * inp_local, slabs * 2 * count)
-    return make_gram(m, slabs * count)
+    tiles = lax.all_to_all(tiles, ("chip", "tm", "core"), split_axis=0, concat_axis=0, tiled=True)
+    return make_gram(tiles.reshape(chips, slabs, CORES * inp_local, 2 * count), slabs * count)
 
 
 def solution(mesh):
+    groups, slabs = mesh.devices.shape
+    split = Mesh(mesh.devices.reshape(groups // CORES, CORES, slabs), ("chip", "core", "tm"))
     return jax.shard_map(
         on_device,
-        mesh=mesh,
-        in_specs=(P("inp", "tm"),),
-        out_specs=P(None, ("inp", "tm"), None, None),
+        mesh=split,
+        in_specs=(P(("chip", "core"), "tm"),),
+        out_specs=P(None, ("chip", "core", "tm"), None, None),
         check_vma=False,
     )

time: 66.8 us -> 65.9 us (0.987)
  blocking collectives: 55.6 us -> 54.5 us
    all_to_all x1, blocking collectives: 55.6 us -> 54.5 us  [on_device(): lax.all_to_all(tiles, ('chip', 'tm', 'core'), split_axis=0, concat_axis=0...]
where the time goes in v4:
time: 65.9 us; the launch traced here: 65.6 us
  blocking collectives  54.5 us (83%)
  Pallas kernels  5.47 us (8%)
  starting transfers between devices  4.82 us (7%)
  local copies, waits for them, and re-layouts  0.8 us (1%)
    all_to_all x1, blocking collectives, on_device(): lax.all_to_all(tiles, ('chip', 'tm', 'core'), split_axis=0, concat_axis=0...  54.5 us
    ppermute x1, starting transfers between devices, on_device(): lax.ppermute(volts[:, samples - (TAPS - 1) * FFT:], 'tm', [(i, i + 1) for...  4.82 us
    pallas_call x1, Pallas kernels, make_gram(): pl.pallas_call(functools.partial(gram_kernel, 1.0 / time_total), out_shap...  2.25 us
    pallas_call x1, Pallas kernels, prepare(): pl.pallas_call(functools.partial(prepare_kernel, count), out_shape=(jax.S...  2.08 us
  transfers between devices with their start and end apart: 1, of which 0 were waited for; matrix products, arithmetic and copies ran while one was open for 0% of the time, Pallas kernels for 3%

profile of v4, /device:TPU:1, one launch (start us, length us, event | category | flops | bytes accessed | tf_op | source)
XLA Modules:
  0.0 65.6 jit_solution(12134944751886701358)
XLA Ops:
  0.0 0.8 %slice.3 = bf16[8,3072]{1,0:T(8,128)(2,1)S(1)} slice(bf16[8,65536]{1,0:T(8,128)(2,1)} %volts_ref.1), slice={[0:8], [62464:65536]} | slice | bytes 98304 | tf_op jit(solution)/shard_map/slice | solution.py:281
  0.8 4.8 %collective-permute-start = (bf16[8,3072]{1,0:T(8,128)(2,1)S(1)}, bf16[8,3072]{1,0:T(8,128)(2,1)S(1)}, u32[]{:S(2)}, u32[]{:S(2)}) collective-permute-start(bf16[8,3072]{1,0:T(8,128)(2,1)S(1)} %slice.3), channel_id=1, source_target_pairs={{0,1},{1,2},{2,3},{3,4},{4,5},{5,6},{6,7},{8,9},{9,10},{10,11},{11... | collective-permute-start | bytes 147464 | tf_op jit(solution)/shard_map/ppermute | solution.py:280
  5.6 2.1 %prepare.1 = (bf16[1024,512]{1,0:T(8,128)(2,1)S(1)}, f32[4,1024]{1,0:T(4,128)S(1)}, bf16[1024,512]{1,0:T(8,128)(2,1)S(1)}, f32[24,1024]{1,0:T(8,128)S(1)}) custom-call(bf16[8,65536]{1,0:T(8,128)(2,1)} %volts_ref.1), custom_call_target="tpu_custom_call" | custom-call | flops 8000000 | bytes 1100000 | tf_op jit(solution)/shard_map/prepare/pallas_call | solution.py:127
  7.7 0.0 collective-permute-done.halo_ref
  7.7 1.1 %spectra.1 = (bf16[4096,128]{1,0:T(8,128)(2,1)S(1)}, bf16[1024,512]{1,0:T(8,128)(2,1)S(1)}) custom-call(bf16[8,3072]{1,0:T(8,128)(2,1)S(1)} %collective-permute-done.halo_ref, f32[4,1024]{1,0:T(4,128)S(1)} %get-tuple-element.10.coef_ref, bf16[1024,512]{1,0:T(8,128)(2,1)S(1)} %get-tuple-element.11.tab_ref, ...), custom_call_target="tpu_custom_call", output_to_operand_aliasing={{1}: (3, {})} | custom-call | flops 540000000 | bytes 3000000 | tf_op jit(solution)/shard_map/spectra/pallas_call | solution.py:207
  8.9 54.5 %all_to_all.5 = bf16[512,8,128]{2,1,0:T(8,128)(2,1)S(1)} all-to-all(bf16[512,8,128]{2,1,0:T(8,128)(2,1)S(1)} %bitcast.2), channel_id=1, replica_groups=mesh['chip'=32,'core'=2,'tm'=8] {'chip','tm','core'}, dimensions={0} | all-to-all | bytes 2097152 | tf_op jit(solution)/shard_map/all_to_all | solution.py:286
  63.4 2.3 %gram.1 = f32[2,1,512,512]{3,2,1,0:T(8,128)} custom-call(bf16[32,8,16,128]{3,2,1,0:T(8,128)(2,1)S(1)} %bitcast.3), custom_call_target="tpu_custom_call" | custom-call | flops 1100000000 | bytes 3200000 | tf_op jit(solution)/shard_map/gram/pallas_call | solution.py:258
Async XLA Ops:
  0.8 6.9 %collective-permute-start = (bf16[8,3072]{1,0:T(8,128)(2,1)S(1)}, bf16[8,3072]{1,0:T(8,128)(2,1)S(1)}, u32[]{:S(2)}, u32[]{:S(2)}) collective-permute-start(bf16[8,3072]{1,0:T(8,128)(2,1)S(1)} %slice.3), channel_id=1, source_target_pairs={{0,1},{1,2},{2,3},{3,4},{4,5},{5,6},{6,7},{8,9},{9,10},{10,11},{11... | collective-permute-start | bytes 147464 | tf_op jit(solution)/shard_map/ppermute | solution.py:280

commit v5 on v2

--- a/solution.py
+++ b/solution.py
@@ -6,6 +6,7 @@
 from jax import lax
 from jax.experimental import pallas as pl
 from jax.experimental.pallas import tpu as pltpu
+from jax.sharding import Mesh
 from jax.sharding import PartitionSpec as P
 
 FFT = 1024
@@ -14,6 +15,7 @@
 LANES = 128
 ROWS = 8
 LOADS = 4
+CORES = 2
 VMEM_LIMIT = 40 * 1024 * 1024
 NT = (((1,), (1,)), ((), ()))
 
@@ -37,38 +39,41 @@
 
     step = 2.0 * math.pi / FFT
     scale = 1.0 / math.sqrt(FFT)
-    groups = CHAN // ROWS
+    groups = CHAN // (2 * ROWS)
     phase = (
         lax.broadcasted_iota(jnp.int32, (groups, LANES), 0)
         * lax.broadcasted_iota(jnp.int32, (groups, LANES), 1)
-        * ROWS
+        * (2 * ROWS)
     ) % FFT
     angle = phase.astype(jnp.float32) * step
     ecos_ref[...] = jnp.cos(angle)
     esin_ref[...] = jnp.sin(angle)
     sub = lax.broadcasted_iota(jnp.int32, (ROWS, LANES), 0)
     lane = lax.broadcasted_iota(jnp.int32, (ROWS, LANES), 1)
-    angle = (sub * lane).astype(jnp.float32) * step
-    gcos = jnp.cos(angle) * scale
-    gsin = jnp.sin(angle) * scale
     half_turns = FFT // LANES // 2
-    turns = []
-    for j in range(half_turns):
-        angle = ((sub * (j * LANES)) % FFT).astype(jnp.float32) * step
-        turns.append((jnp.cos(angle), jnp.sin(angle)))
-    odd = lax.broadcasted_iota(jnp.int32, (2 * ROWS, LANES), 0) % 2 == 1
+    factors = []
+    for h in range(2):
+        near = ROWS * (sub % CORES) + sub // CORES + h * ROWS // 2
+        angle = ((near * lane) % FFT).astype(jnp.float32) * step
+        turns = []
+        for j in range(half_turns):
+            turn = ((near * (j * LANES)) % FFT).astype(jnp.float32) * step
+            turns.append((jnp.cos(turn), jnp.sin(turn)))
+        factors.append((jnp.cos(angle) * scale, jnp.sin(angle) * scale, turns))
+    odd = lax.broadcasted_iota(jnp.int32, (2 * ROWS, LANES), 0) // CORES % 2 == 1
     sign = jnp.where(odd, -1.0, 1.0).astype(jnp.bfloat16)
 
-    def pair(p, carry):
-        bases = []
-        for half in range(2):
-            ec = ecos_ref[pl.ds(2 * p + half, 1), :]
-            es = esin_ref[pl.ds(2 * p + half, 1), :]
-            bases.append((ec * gcos - es * gsin, es * gcos + ec * gsin))
-        row = pl.multiple_of(p * 2 * ROWS, 2 * ROWS)
-        for j, (tc, ts) in enumerate(turns):
-            real = [bc * tc - bs * ts for bc, bs in bases] if j else [bc for bc, bs in bases]
-            imag = [-(bs * tc + bc * ts) for bc, bs in bases] if j else [-bs for bc, bs in bases]
+    def pair(w, carry):
+        ec = ecos_ref[pl.ds(w, 1), :]
+        es = esin_ref[pl.ds(w, 1), :]
+        bases = [(ec * gcos - es * gsin, es * gcos + ec * gsin) for gcos, gsin, _ in factors]
+        row = pl.multiple_of(w * 2 * ROWS, 2 * ROWS)
+        for j in range(half_turns):
+            real, imag = [], []
+            for (bc, bs), (_, _, turns) in zip(bases, factors):
+                tc, ts = turns[j]
+                real.append(bc * tc - bs * ts if j else bc)
+                imag.append(-(bs * tc + bc * ts) if j else -bs)
             for q, value in enumerate((real, imag)):
                 value = jnp.concatenate(value, 0).astype(jnp.bfloat16)
                 rows = pl.ds(q * CHAN + row, 2 * ROWS)
@@ -76,7 +81,7 @@
                 tab_ref[rows, (j + half_turns) * LANES : (j + half_turns + 1) * LANES] = value * sign
         return carry
 
-    lax.fori_loop(0, groups // 2, pair, 0)
+    lax.fori_loop(0, groups, pair, 0)
 
     for load in loads:
         load.wait()
@@ -124,8 +129,8 @@
         scratch_shapes=[
             pltpu.VMEM((ROWS, samples), jnp.bfloat16),
             pltpu.VMEM((ROWS * (count + ROWS), LANES), jnp.float32),
-            pltpu.VMEM((CHAN // ROWS, LANES), jnp.float32),
-            pltpu.VMEM((CHAN // ROWS, LANES), jnp.float32),
+            pltpu.VMEM((CHAN // (2 * ROWS), LANES), jnp.float32),
+            pltpu.VMEM((CHAN // (2 * ROWS), LANES), jnp.float32),
             pltpu.SemaphoreType.DMA((LOADS,)),
         ],
         compiler_params=pltpu.CompilerParams(vmem_limit_bytes=VMEM_LIMIT),
@@ -198,13 +203,15 @@
     )(halo, coef, table, filtered, head)[0]
 
 
-def gram_kernel(scale, m_ref, out_ref, turned_ref, block_ref, sem):
+def gram_kernel(scale, tiles_ref, out_ref, m_ref, turned_ref, block_ref, sem):
     inputs, depth = m_ref.shape
     block = inputs // 2
     low = lax.broadcasted_iota(jnp.int32, (inputs, LANES), 1) < LANES // 2
     for k in range(depth // LANES):
         cols = slice(k * LANES, (k + 1) * LANES)
-        swapped = pltpu.roll(m_ref[:, cols], LANES // 2, 1)
+        tile = tiles_ref[:, k].reshape(inputs, LANES)
+        m_ref[:, cols] = tile
+        swapped = pltpu.roll(tile, LANES // 2, 1)
         turned_ref[:, cols] = jnp.where(low, -swapped, swapped)
     copies = []
     for i in range(2):
@@ -224,8 +231,9 @@
         copy.wait()
 
 
-def make_gram(m, time_total):
-    inputs, depth = m.shape
+def make_gram(tiles, time_total):
+    chips, slabs, rows, lanes = tiles.shape
+    inputs, depth = chips * rows, slabs * lanes
     shape = (2, 1, inputs, inputs)
     return pl.pallas_call(
         functools.partial(gram_kernel, 1.0 / time_total),
@@ -234,37 +242,38 @@
         out_specs=pl.BlockSpec(memory_space=pl.ANY),
         scratch_shapes=[
             pltpu.VMEM((inputs, depth), jnp.bfloat16),
+            pltpu.VMEM((inputs, depth), jnp.bfloat16),
             pltpu.VMEM(shape, jnp.float32),
             pltpu.SemaphoreType.DMA((4,)),
         ],
         compiler_params=pltpu.CompilerParams(vmem_limit_bytes=VMEM_LIMIT),
         cost_estimate=pl.CostEstimate(flops=1_100_000_000, bytes_accessed=3_200_000, transcendentals=0),
         name="gram",
-    )(m)
+    )(tiles)
 
 
 def on_device(volts):
     inp_local, samples = volts.shape
     count = samples // FFT
     slabs = lax.axis_size("tm")
-    groups = lax.axis_size("inp")
+    chips = lax.axis_size("chip")
     halo = lax.ppermute(
         volts[:, samples - (TAPS - 1) * FFT :], "tm", [(i, i + 1) for i in range(slabs - 1)]
     )
     table, coef, filtered, head = prepare(volts)
     tiles = make_spectra(halo, coef, table, filtered, head)
     tiles = tiles.reshape(CHAN, inp_local, 2 * count)
-    tiles = lax.all_to_all(tiles, ("inp", "tm"), split_axis=0, concat_axis=0, tiled=True)
-    m = tiles.reshape(groups, slabs, inp_local, 2 * count).transpose(0, 2, 1, 3)
-    m = m.reshape(groups * inp_local, slabs * 2 * count)
-    return make_gram(m, slabs * count)
+    tiles = lax.all_to_all(tiles, ("chip", "tm", "core"), split_axis=0, concat_axis=0, tiled=True)
+    return make_gram(tiles.reshape(chips, slabs, CORES * inp_local, 2 * count), slabs * count)
 
 
 def solution(mesh):
+    groups, slabs = mesh.devices.shape
+    split = Mesh(mesh.devices.reshape(groups // CORES, CORES, slabs), ("chip", "core", "tm"))
     return jax.shard_map(
         on_device,
-        mesh=mesh,
-        in_specs=(P("inp", "tm"),),
-        out_specs=P(None, ("inp", "tm"), None, None),
+        mesh=split,
+        in_specs=(P(("chip", "core"), "tm"),),
+        out_specs=P(None, ("chip", "core", "tm"), None, None),
         check_vma=False,
     )

time: 67.4 us -> 66.4 us (0.985)
  blocking collectives: 55.5 us -> 54.4 us
    all_to_all x1, blocking collectives: 55.5 us -> 54.4 us  [on_device(): lax.all_to_all(tiles, ('chip', 'tm', 'core'), split_axis=0, concat_axis=0...]
where the time goes in v5:
time: 66.4 us; the launch traced here: 66.2 us
  blocking collectives  54.4 us (82%)
  Pallas kernels  6.1 us (9%)
  starting transfers between devices  4.82 us (7%)
  local copies, waits for them, and re-layouts  0.8 us (1%)
    all_to_all x1, blocking collectives, on_device(): lax.all_to_all(tiles, ('chip', 'tm', 'core'), split_axis=0, concat_axis=0...  54.4 us
    ppermute x1, starting transfers between devices, on_device(): lax.ppermute(volts[:, samples - (TAPS - 1) * FFT:], 'tm', [(i, i + 1) for...  4.82 us
    pallas_call x1, Pallas kernels, make_gram(): pl.pallas_call(functools.partial(gram_kernel, 1.0 / time_total), out_shap...  2.26 us
    pallas_call x1, Pallas kernels, prepare(): pl.pallas_call(functools.partial(prepare_kernel, count), out_shape=(jax.S...  2.18 us
    pallas_call x1, Pallas kernels, make_spectra(): pl.pallas_call(functools.partial(spectra_kernel, count), out_shape=(jax.S...  1.67 us
  transfers between devices with their start and end apart: 1, of which 0 were waited for; matrix products, arithmetic and copies ran while one was open for 0% of the time, Pallas kernels for 3%

profile of v5, /device:TPU:1, one launch (start us, length us, event | category | flops | bytes accessed | tf_op | source)
XLA Modules:
  0.0 66.2 jit_solution(269014607961808542)
XLA Ops:
  0.0 0.8 %slice.3 = bf16[8,3072]{1,0:T(8,128)(2,1)S(1)} slice(bf16[8,65536]{1,0:T(8,128)(2,1)} %volts_ref.1), slice={[0:8], [62464:65536]} | slice | bytes 98304 | tf_op jit(solution)/shard_map/slice | solution.py:261
  0.8 4.8 %collective-permute-start = (bf16[8,3072]{1,0:T(8,128)(2,1)S(1)}, bf16[8,3072]{1,0:T(8,128)(2,1)S(1)}, u32[]{:S(2)}, u32[]{:S(2)}) collective-permute-start(bf16[8,3072]{1,0:T(8,128)(2,1)S(1)} %slice.3), channel_id=1, source_target_pairs={{0,1},{1,2},{2,3},{3,4},{4,5},{5,6},{6,7},{8,9},{9,10},{10,11},{11... | collective-permute-start | bytes 147464 | tf_op jit(solution)/shard_map/ppermute | solution.py:260
  5.6 2.2 %prepare.1 = (bf16[1024,1024]{1,0:T(8,128)(2,1)S(1)}, f32[4,1024]{1,0:T(4,128)S(1)}, bf16[512,1024]{1,0:T(8,128)(2,1)S(1)}, f32[24,1024]{1,0:T(8,128)S(1)}) custom-call(bf16[8,65536]{1,0:T(8,128)(2,1)} %volts_ref.1), custom_call_target="tpu_custom_call" | custom-call | flops 8000000 | bytes 1100000 | tf_op jit(solution)/shard_map/prepare/pallas_call | solution.py:119
  7.8 0.0 collective-permute-done.halo_ref
  7.8 1.7 %spectra.1 = (bf16[4096,128]{1,0:T(8,128)(2,1)S(1)}, bf16[512,1024]{1,0:T(8,128)(2,1)S(1)}) custom-call(bf16[8,3072]{1,0:T(8,128)(2,1)S(1)} %collective-permute-done.halo_ref, f32[4,1024]{1,0:T(4,128)S(1)} %get-tuple-element.10.coef_ref, bf16[1024,1024]{1,0:T(8,128)(2,1)S(1)} %get-tuple-element.11.tab_ref, ...), custom_call_target="tpu_custom_call", output_to_operand_aliasing={{1}: (3, {})} | custom-call | flops 1100000000 | bytes 4000000 | tf_op jit(solution)/shard_map/spectra/pallas_call | solution.py:187
  9.5 54.4 %all_to_all.5 = bf16[512,8,128]{2,1,0:T(8,128)(2,1)S(1)} all-to-all(bf16[512,8,128]{2,1,0:T(8,128)(2,1)S(1)} %bitcast.2), channel_id=1, replica_groups=mesh['chip'=32,'core'=2,'tm'=8] {'chip','tm','core'}, dimensions={0} | all-to-all | bytes 2097152 | tf_op jit(solution)/shard_map/all_to_all | solution.py:266
  63.9 2.3 %gram.1 = f32[2,1,512,512]{3,2,1,0:T(8,128)} custom-call(bf16[32,8,16,128]{3,2,1,0:T(8,128)(2,1)S(1)} %bitcast.3), custom_call_target="tpu_custom_call" | custom-call | flops 1100000000 | bytes 3200000 | tf_op jit(solution)/shard_map/gram/pallas_call | solution.py:238
Async XLA Ops:
  0.8 7.0 %collective-permute-start = (bf16[8,3072]{1,0:T(8,128)(2,1)S(1)}, bf16[8,3072]{1,0:T(8,128)(2,1)S(1)}, u32[]{:S(2)}, u32[]{:S(2)}) collective-permute-start(bf16[8,3072]{1,0:T(8,128)(2,1)S(1)} %slice.3), channel_id=1, source_target_pairs={{0,1},{1,2},{2,3},{3,4},{4,5},{5,6},{6,7},{8,9},{9,10},{10,11},{11... | collective-permute-start | bytes 147464 | tf_op jit(solution)/shard_map/ppermute | solution.py:260

commit v6 on v4

--- a/solution.py
+++ b/solution.py
@@ -136,7 +136,7 @@
         out_specs=(vmem,) * 4,
         scratch_shapes=[
             pltpu.VMEM((ROWS, samples), jnp.bfloat16),
-            pltpu.VMEM((2 * ROWS * (count + ROWS), LANES), jnp.float32),
+            pltpu.VMEM(((2 * ROWS + 1) * (count + ROWS), LANES), jnp.float32),
             pltpu.VMEM((CHAN // 2 // ROWS, LANES), jnp.float32),
             pltpu.VMEM((CHAN // 2 // ROWS, LANES), jnp.float32),
             pltpu.SemaphoreType.DMA((LOADS,)),
@@ -197,7 +197,7 @@
             )
     pairs = (chunk // CORES, 1, CORES * ROWS, LANES)
     even = tile_ref[: chunk * ROWS, :].reshape(pairs)
-    odd = tile_ref[chunk * ROWS :, :].reshape(pairs)
+    odd = tile_ref[chunk * ROWS : CHAN * ROWS, :].reshape(pairs)
     out_ref[...] = jnp.concatenate([even, odd], 1).reshape(CHAN * ROWS, LANES).astype(jnp.bfloat16)
 
 
@@ -214,8 +214,8 @@
         out_specs=(vmem, vmem),
         input_output_aliases={3: 1},
         scratch_shapes=[
-            pltpu.VMEM((2 * ROWS * ROWS, LANES), jnp.float32),
-            pltpu.VMEM((CHAN * ROWS, LANES), jnp.float32),
+            pltpu.VMEM(((2 * ROWS + 1) * ROWS, LANES), jnp.float32),
+            pltpu.VMEM(((CHAN + 1) * ROWS, LANES), jnp.float32),
         ],
         compiler_params=pltpu.CompilerParams(vmem_limit_bytes=VMEM_LIMIT),
         cost_estimate=pl.CostEstimate(flops=540_000_000, bytes_accessed=3_000_000, transcendentals=0),

time: 65.9 us -> 65.9 us (level)
  no operation moved by 1% of the time
where the time goes in v6:
time: 65.9 us; the launch traced here: 65.7 us
  blocking collectives  54.5 us (83%)
  Pallas kernels  5.48 us (8%)
  starting transfers between devices  4.82 us (7%)
  local copies, waits for them, and re-layouts  0.8 us (1%)
    all_to_all x1, blocking collectives, on_device(): lax.all_to_all(tiles, ('chip', 'tm', 'core'), split_axis=0, concat_axis=0...  54.5 us
    ppermute x1, starting transfers between devices, on_device(): lax.ppermute(volts[:, samples - (TAPS - 1) * FFT:], 'tm', [(i, i + 1) for...  4.82 us
    pallas_call x1, Pallas kernels, make_gram(): pl.pallas_call(functools.partial(gram_kernel, 1.0 / time_total), out_shap...  2.26 us
    pallas_call x1, Pallas kernels, prepare(): pl.pallas_call(functools.partial(prepare_kernel, count), out_shape=(jax.S...  2.08 us
  transfers between devices with their start and end apart: 1, of which 0 were waited for; matrix products, arithmetic and copies ran while one was open for 0% of the time, Pallas kernels for 3%

profile of v6, /device:TPU:1, one launch (start us, length us, event | category | flops | bytes accessed | tf_op | source)
XLA Modules:
  0.0 65.7 jit_solution(8780298521106553626)
XLA Ops:
  0.0 0.8 %slice.3 = bf16[8,3072]{1,0:T(8,128)(2,1)S(1)} slice(bf16[8,65536]{1,0:T(8,128)(2,1)} %volts_ref.1), slice={[0:8], [62464:65536]} | slice | bytes 98304 | tf_op jit(solution)/shard_map/slice | solution.py:281
  0.8 4.8 %collective-permute-start = (bf16[8,3072]{1,0:T(8,128)(2,1)S(1)}, bf16[8,3072]{1,0:T(8,128)(2,1)S(1)}, u32[]{:S(2)}, u32[]{:S(2)}) collective-permute-start(bf16[8,3072]{1,0:T(8,128)(2,1)S(1)} %slice.3), channel_id=1, source_target_pairs={{0,1},{1,2},{2,3},{3,4},{4,5},{5,6},{6,7},{8,9},{9,10},{10,11},{11... | collective-permute-start | bytes 147464 | tf_op jit(solution)/shard_map/ppermute | solution.py:280
  5.6 2.1 %prepare.1 = (bf16[1024,512]{1,0:T(8,128)(2,1)S(1)}, f32[4,1024]{1,0:T(4,128)S(1)}, bf16[1024,512]{1,0:T(8,128)(2,1)S(1)}, f32[24,1024]{1,0:T(8,128)S(1)}) custom-call(bf16[8,65536]{1,0:T(8,128)(2,1)} %volts_ref.1), custom_call_target="tpu_custom_call" | custom-call | flops 8000000 | bytes 1100000 | tf_op jit(solution)/shard_map/prepare/pallas_call | solution.py:127
  7.7 0.0 collective-permute-done.halo_ref
  7.7 1.1 %spectra.1 = (bf16[4096,128]{1,0:T(8,128)(2,1)S(1)}, bf16[1024,512]{1,0:T(8,128)(2,1)S(1)}) custom-call(bf16[8,3072]{1,0:T(8,128)(2,1)S(1)} %collective-permute-done.halo_ref, f32[4,1024]{1,0:T(4,128)S(1)} %get-tuple-element.10.coef_ref, bf16[1024,512]{1,0:T(8,128)(2,1)S(1)} %get-tuple-element.11.tab_ref, ...), custom_call_target="tpu_custom_call", output_to_operand_aliasing={{1}: (3, {})} | custom-call | flops 540000000 | bytes 3000000 | tf_op jit(solution)/shard_map/spectra/pallas_call | solution.py:207
  8.9 54.5 %all_to_all.5 = bf16[512,8,128]{2,1,0:T(8,128)(2,1)S(1)} all-to-all(bf16[512,8,128]{2,1,0:T(8,128)(2,1)S(1)} %bitcast.2), channel_id=1, replica_groups=mesh['chip'=32,'core'=2,'tm'=8] {'chip','tm','core'}, dimensions={0} | all-to-all | bytes 2097152 | tf_op jit(solution)/shard_map/all_to_all | solution.py:286
  63.4 2.3 %gram.1 = f32[2,1,512,512]{3,2,1,0:T(8,128)} custom-call(bf16[32,8,16,128]{3,2,1,0:T(8,128)(2,1)S(1)} %bitcast.3), custom_call_target="tpu_custom_call" | custom-call | flops 1100000000 | bytes 3200000 | tf_op jit(solution)/shard_map/gram/pallas_call | solution.py:258
Async XLA Ops:
  0.8 6.9 %collective-permute-start = (bf16[8,3072]{1,0:T(8,128)(2,1)S(1)}, bf16[8,3072]{1,0:T(8,128)(2,1)S(1)}, u32[]{:S(2)}, u32[]{:S(2)}) collective-permute-start(bf16[8,3072]{1,0:T(8,128)(2,1)S(1)} %slice.3), channel_id=1, source_target_pairs={{0,1},{1,2},{2,3},{3,4},{4,5},{5,6},{6,7},{8,9},{9,10},{10,11},{11... | collective-permute-start | bytes 147464 | tf_op jit(solution)/shard_map/ppermute | solution.py:280

commit v7 on v5

--- a/solution.py
+++ b/solution.py
@@ -128,7 +128,7 @@
         out_specs=(vmem,) * 4,
         scratch_shapes=[
             pltpu.VMEM((ROWS, samples), jnp.bfloat16),
-            pltpu.VMEM((ROWS * (count + ROWS), LANES), jnp.float32),
+            pltpu.VMEM(((ROWS + 1) * (count + ROWS), LANES), jnp.float32),
             pltpu.VMEM((CHAN // (2 * ROWS), LANES), jnp.float32),
             pltpu.VMEM((CHAN // (2 * ROWS), LANES), jnp.float32),
             pltpu.SemaphoreType.DMA((LOADS,)),
@@ -178,7 +178,9 @@
             tile_ref[pl.ds(2 * j + 1, chunk, stride=ROWS), :] = jnp.where(
                 low, pltpu.roll(re, LANES // 2, 1), im
             )
-        out_ref[h * chunk * ROWS : (h + 1) * chunk * ROWS, :] = tile_ref[...].astype(jnp.bfloat16)
+        out_ref[h * chunk * ROWS : (h + 1) * chunk * ROWS, :] = tile_ref[: chunk * ROWS, :].astype(
+            jnp.bfloat16
+        )
 
 
 def make_spectra(halo, coef, table, filtered, head):
@@ -194,8 +196,8 @@
         out_specs=(vmem, vmem),
         input_output_aliases={3: 1},
         scratch_shapes=[
-            pltpu.VMEM((ROWS * ROWS, LANES), jnp.float32),
-            pltpu.VMEM((256 * ROWS, LANES), jnp.float32),
+            pltpu.VMEM(((ROWS + 1) * ROWS, LANES), jnp.float32),
+            pltpu.VMEM((257 * ROWS, LANES), jnp.float32),
         ],
         compiler_params=pltpu.CompilerParams(vmem_limit_bytes=VMEM_LIMIT),
         cost_estimate=pl.CostEstimate(flops=1_100_000_000, bytes_accessed=4_000_000, transcendentals=0),

time: 66.4 us -> 66.4 us (level)
  no operation moved by 1% of the time
where the time goes in v7:
time: 66.4 us; the launch traced here: 66.2 us
  blocking collectives  54.4 us (82%)
  Pallas kernels  6.11 us (9%)
  starting transfers between devices  4.82 us (7%)
  local copies, waits for them, and re-layouts  0.8 us (1%)
    all_to_all x1, blocking collectives, on_device(): lax.all_to_all(tiles, ('chip', 'tm', 'core'), split_axis=0, concat_axis=0...  54.4 us
    ppermute x1, starting transfers between devices, on_device(): lax.ppermute(volts[:, samples - (TAPS - 1) * FFT:], 'tm', [(i, i + 1) for...  4.82 us
    pallas_call x1, Pallas kernels, make_gram(): pl.pallas_call(functools.partial(gram_kernel, 1.0 / time_total), out_shap...  2.26 us
    pallas_call x1, Pallas kernels, prepare(): pl.pallas_call(functools.partial(prepare_kernel, count), out_shape=(jax.S...  2.18 us
    pallas_call x1, Pallas kernels, make_spectra(): pl.pallas_call(functools.partial(spectra_kernel, count), out_shape=(jax.S...  1.68 us
  transfers between devices with their start and end apart: 1, of which 0 were waited for; matrix products, arithmetic and copies ran while one was open for 0% of the time, Pallas kernels for 3%

profile of v7, /device:TPU:1, one launch (start us, length us, event | category | flops | bytes accessed | tf_op | source)
XLA Modules:
  0.0 66.2 jit_solution(13910847865327061551)
XLA Ops:
  0.0 0.8 %slice.3 = bf16[8,3072]{1,0:T(8,128)(2,1)S(1)} slice(bf16[8,65536]{1,0:T(8,128)(2,1)} %volts_ref.1), slice={[0:8], [62464:65536]} | slice | bytes 98304 | tf_op jit(solution)/shard_map/slice | solution.py:263
  0.8 4.8 %collective-permute-start = (bf16[8,3072]{1,0:T(8,128)(2,1)S(1)}, bf16[8,3072]{1,0:T(8,128)(2,1)S(1)}, u32[]{:S(2)}, u32[]{:S(2)}) collective-permute-start(bf16[8,3072]{1,0:T(8,128)(2,1)S(1)} %slice.3), channel_id=1, source_target_pairs={{0,1},{1,2},{2,3},{3,4},{4,5},{5,6},{6,7},{8,9},{9,10},{10,11},{11... | collective-permute-start | bytes 147464 | tf_op jit(solution)/shard_map/ppermute | solution.py:262
  5.6 2.2 %prepare.1 = (bf16[1024,1024]{1,0:T(8,128)(2,1)S(1)}, f32[4,1024]{1,0:T(4,128)S(1)}, bf16[512,1024]{1,0:T(8,128)(2,1)S(1)}, f32[24,1024]{1,0:T(8,128)S(1)}) custom-call(bf16[8,65536]{1,0:T(8,128)(2,1)} %volts_ref.1), custom_call_target="tpu_custom_call" | custom-call | flops 8000000 | bytes 1100000 | tf_op jit(solution)/shard_map/prepare/pallas_call | solution.py:119
  7.8 0.0 collective-permute-done.halo_ref
  7.8 1.7 %spectra.1 = (bf16[4096,128]{1,0:T(8,128)(2,1)S(1)}, bf16[512,1024]{1,0:T(8,128)(2,1)S(1)}) custom-call(bf16[8,3072]{1,0:T(8,128)(2,1)S(1)} %collective-permute-done.halo_ref, f32[4,1024]{1,0:T(4,128)S(1)} %get-tuple-element.10.coef_ref, bf16[1024,1024]{1,0:T(8,128)(2,1)S(1)} %get-tuple-element.11.tab_ref, ...), custom_call_target="tpu_custom_call", output_to_operand_aliasing={{1}: (3, {})} | custom-call | flops 1100000000 | bytes 4000000 | tf_op jit(solution)/shard_map/spectra/pallas_call | solution.py:189
  9.5 54.4 %all_to_all.5 = bf16[512,8,128]{2,1,0:T(8,128)(2,1)S(1)} all-to-all(bf16[512,8,128]{2,1,0:T(8,128)(2,1)S(1)} %bitcast.2), channel_id=1, replica_groups=mesh['chip'=32,'core'=2,'tm'=8] {'chip','tm','core'}, dimensions={0} | all-to-all | bytes 2097152 | tf_op jit(solution)/shard_map/all_to_all | solution.py:268
  63.9 2.3 %gram.1 = f32[2,1,512,512]{3,2,1,0:T(8,128)} custom-call(bf16[32,8,16,128]{3,2,1,0:T(8,128)(2,1)S(1)} %bitcast.3), custom_call_target="tpu_custom_call" | custom-call | flops 1100000000 | bytes 3200000 | tf_op jit(solution)/shard_map/gram/pallas_call | solution.py:240
Async XLA Ops:
  0.8 7.0 %collective-permute-start = (bf16[8,3072]{1,0:T(8,128)(2,1)S(1)}, bf16[8,3072]{1,0:T(8,128)(2,1)S(1)}, u32[]{:S(2)}, u32[]{:S(2)}) collective-permute-start(bf16[8,3072]{1,0:T(8,128)(2,1)S(1)} %slice.3), channel_id=1, source_target_pairs={{0,1},{1,2},{2,3},{3,4},{4,5},{5,6},{6,7},{8,9},{9,10},{10,11},{11... | collective-permute-start | bytes 147464 | tf_op jit(solution)/shard_map/ppermute | solution.py:262
